TPU v7x, 256 devices: a whole 4x4x8 slice. The times are simulated.
256 devices in a mesh: ctx: 8 (over x_hi, y), fsdp: 32 (over x_lo, z, core).
Axes of the slice: x: 4 (x_hi: 2, x_lo: 2; x = x_hi * 2 + x_lo), y: 4, z: 8, core: 2. Of those that a mesh axis runs over, the one named last changes fastest.
Arguments:
- base_ids: int32 [3072], P('ctx'), may hold values from 0 to 511
- embedding: bfloat16 [512, 8192], P(None, 'fsdp'), may hold values from -3 to 3
- first_gain: float32 [8192], replicated, may hold values from 0.1 to 1.9
- hyena_weight: bfloat16 [8192, 3, 8192], P('ctx', None, 'fsdp'), may hold values from -0.0625 to 0.0625
- short_filter: float32 [3, 3, 8192], P(None, None, 'fsdp'), may hold values from -3 to 3
- long_filter: float32 [128, 8192], P(None, 'fsdp'), may hold values from -0.5 to 0.5
- second_gain: float32 [8192], replicated, may hold values from 0.1 to 1.9
- attn_weight: bfloat16 [8192, 3, 8192], P('ctx', None, 'fsdp'), may hold values from -0.0625 to 0.0625
Outputs:
- mixed: bfloat16 [3072, 8192], P('ctx', 'fsdp')
- attended: bfloat16 [3072, 8192], P('ctx', 'fsdp')
All inputs are finite; a program needn't handle non-finite values.
Results may differ from a plain program's by a relative error of at most 0.02.
Values may be sent and summed in bfloat16 or wider, within the bound.
A program may use at most 64 MiB of HBM per device.

v0:
```python
import jax
import jax.numpy as jnp
from jax import lax
from jax.sharding import PartitionSpec as P

HEAD = 128


def shifted(shard, axis, by):
    count = lax.axis_size(axis)
    pairs = [(i, i + by) for i in range(count) if 0 <= i + by < count]
    return lax.ppermute(shard, axis, pairs)


def norm_rows(values, gain_vector):
    values = values.astype(jnp.float32)
    factor = lax.rsqrt(jnp.mean(values * values, axis=-1, keepdims=True) + 1e-06)
    return values * factor * gain_vector


def head_norm(values):
    values = values.astype(jnp.float32)
    return values * lax.rsqrt(jnp.mean(values * values, axis=-1, keepdims=True) + 1e-06)


def depthwise(values, kernel):
    flipped = kernel[::-1][:, None, :]
    result = lax.conv_general_dilated(
        values[None],
        flipped,
        (1,),
        "VALID",
        dimension_numbers=("NWC", "WIO", "NWC"),
        feature_group_count=values.shape[1],
        precision=lax.Precision.HIGHEST,
    )
    return result[0]


def add_rows(running, normed, segment):
    columns = lax.slice_in_dim(normed, 0, segment.shape[0], axis=1)
    return running + jnp.einsum("td,dmc->tmc", columns, segment, preferred_element_type=jnp.float32)


def local(
    base_ids,
    embedding,
    first_gain,
    hyena_weight,
    short_filter,
    long_filter,
    second_gain,
    attn_weight,
):
    length = base_ids.shape[0]
    channels = embedding.shape[1]
    short_taps = short_filter.shape[0]
    long_taps = long_filter.shape[0]
    vocab_iota = lax.broadcasted_iota(jnp.int32, (length, embedding.shape[0]), 1)
    one_hot = (base_ids[:, None] == vocab_iota).astype(jnp.bfloat16)
    features = jnp.dot(one_hot, embedding, preferred_element_type=jnp.float32).astype(jnp.bfloat16)
    whole_rows = lax.all_gather(features, "fsdp", axis=1, tiled=True)
    normed = norm_rows(whole_rows, first_gain).astype(jnp.bfloat16)
    empty = jnp.zeros((length, 3, channels), jnp.float32)
    streams = add_rows(empty, normed, lax.all_gather(hyena_weight, "ctx", axis=0, tiled=True))
    flat_streams = streams.astype(jnp.bfloat16).reshape(length, 3 * channels)
    short_kernel = short_filter.reshape(short_taps, 3 * channels)
    edge_rows = shifted(flat_streams[length - (short_taps - 1) :], "ctx", 1)
    filtered = depthwise(
        jnp.concatenate([edge_rows, flat_streams], axis=0).astype(jnp.float32), short_kernel
    )
    filtered = filtered.reshape(length, 3, channels)
    product = (filtered[:, 1, :] * filtered[:, 2, :]).astype(jnp.bfloat16)
    tail_rows = shifted(product[length - (long_taps - 1) :], "ctx", 1)
    extended = jnp.concatenate([tail_rows, product], axis=0)
    query_gate = filtered[:, 0, :]
    longconv = depthwise(extended.astype(jnp.float32), long_filter)
    mixed = (features.astype(jnp.float32) + query_gate * longconv).astype(jnp.bfloat16)
    stream_whole = lax.all_gather(mixed, "fsdp", axis=1, tiled=True)
    renormed = norm_rows(stream_whole, second_gain).astype(jnp.bfloat16)
    triple = add_rows(empty, renormed, lax.all_gather(attn_weight, "ctx", axis=0, tiled=True))
    triple = triple.astype(jnp.bfloat16)
    head_count = channels // HEAD
    unit_q = head_norm(triple[:, 0, :].reshape(length, head_count, HEAD)).astype(jnp.bfloat16)
    unit_k = head_norm(triple[:, 1, :].reshape(length, head_count, HEAD)).astype(jnp.bfloat16)
    values_in = triple[:, 2, :].reshape(length, head_count, HEAD)
    positions = lax.axis_index("ctx") * length + lax.broadcasted_iota(jnp.int32, (length,), 0)
    score_factor = 2.0 * HEAD ** (-0.5)
    key_block = lax.all_gather(unit_k, "ctx", axis=0, tiled=True)
    value_block = lax.all_gather(values_in, "ctx", axis=0, tiled=True)
    score = (
        jnp.einsum("thd,shd->hts", unit_q, key_block, preferred_element_type=jnp.float32)
        * score_factor
    )
    key_positions = lax.broadcasted_iota(jnp.int32, (key_block.shape[0],), 0)
    allowed = key_positions[None, :] <= positions[:, None]
    weight = jnp.where(allowed[None], jnp.exp(score), 0.0)
    numerator = jnp.einsum(
        "hts,shd->thd", weight.astype(jnp.bfloat16), value_block, preferred_element_type=jnp.float32
    )
    denominator = jnp.sum(weight, axis=2).T
    numerator, denominator = (numerator, denominator)
    attended = (numerator / denominator[:, :, None]).reshape(length, channels).astype(jnp.bfloat16)
    return (mixed, attended)


def solution(mesh):
    return jax.shard_map(
        local,
        mesh=mesh,
        in_specs=(
            P("ctx"),
            P(None, "fsdp"),
            P(),
            P("ctx", None, "fsdp"),
            P(None, None, "fsdp"),
            P(None, "fsdp"),
            P(),
            P("ctx", None, "fsdp"),
        ),
        out_specs=(P("ctx", "fsdp"), P("ctx", "fsdp")),
        check_vma=False,
    )
```

profile of v0, /device:TPU:28, one launch (start us, length us, event | category | flops | bytes accessed | tf_op | source)
XLA Modules:
  0.0 646.1 jit_solution(5183521975762579304)
XLA Ops:
  7.2 0.9 copy-done
  8.1 1.7 convolution_convert_fusion
  9.9 0.7 all-gather.9.cloned.1.call-update
  10.6 83.0 %all-gather.7.cloned.1.call-done = bf16[384,8192]{1,0:T(8,128)(2,1)} async-done(((bf16[384,256]{1,0:T(8,128)(2,1)}), bf16[384,8192]{1,0:T(8,128)(2,1)}) %all-gather.7.cloned.1.call-update) | async-done | bytes 6291472 | tf_op jit(solution)/shard_map/all_gather | solution.py:62
  93.6 4.1 fusion
  97.7 142.3 %all-gather.9.cloned.1.call-done = bf16[8192,3,256]{2,0,1:T(8,128)(2,1)} async-done(((bf16[1024,3,256]{2,0,1:T(8,128)(2,1)}), bf16[8192,3,256]{2,0,1:T(8,128)(2,1)}) %all-gather.9.cloned.1.call-update) | async-done | bytes 12582928 | tf_op jit(solution)/shard_map/all_gather | solution.py:65
  240.0 10.9 %fusion.23 = bf16[384,3,256]{2,0,1:T(8,128)(2,1)S(1)} fusion(bf16[8192,3,256]{2,0,1:T(8,128)(2,1)} %all-gather.9.cloned.1.call-done, bf16[384,8192]{1,0:T(8,128)(2,1)} %all-gather.7.cloned.1.call-done, f32[8192]{0:T(1024)S(1)} %copy-done.6, f32[384]{0:T(512)S(1)} %add_rsqrt_fusion.3), kind=kOutput, calls=%fused_computation.27 | convolution fusion | flops 4844716032 | bytes 19498496 | tf_op jit(solution)/shard_map/td,dmc->tmc/dot_general | solution.py:42
  251.0 1.3 collective-permute-start
  252.8 3.7 collective-permute-done
  256.7 0.4 maximum_bitcast_fusion
  258.1 0.4 copy.35
  258.7 1.1 slice.44
  259.8 1.6 copy.36
  261.6 1.3 collective-permute-start.1
  263.2 4.6 collective-permute-done.1
  267.9 0.7 copy.39
  268.7 4.3 fusion.52
  273.0 0.8 fusion.47
  273.8 1.7 copy.41
  275.8 87.2 %all-gather.11.cloned.1.call-done = bf16[384,8192]{1,0:T(8,128)(2,1)} async-done(((bf16[384,256]{1,0:T(8,128)(2,1)}), bf16[384,8192]{1,0:T(8,128)(2,1)}) %all-gather.11.cloned.1.call-update) | async-done | bytes 6291472 | tf_op jit(solution)/shard_map/all_gather | solution.py:79
  363.1 4.1 fusion.3
  367.2 142.2 %all-gather.13.cloned.1.call-done = bf16[8192,3,256]{0,2,1:T(8,128)(2,1)} async-done(((bf16[1024,3,256]{0,2,1:T(8,128)(2,1)}), bf16[8192,3,256]{0,2,1:T(8,128)(2,1)}) %all-gather.13.cloned.1.call-update) | async-done | bytes 12582928 | tf_op jit(solution)/shard_map/all_gather | solution.py:81
  509.3 11.7 %fusion.26 = bf16[384,3,256]{0,2,1:T(8,128)(2,1)S(1)} fusion(bf16[8192,3,256]{0,2,1:T(8,128)(2,1)} %all-gather.13.cloned.1.call-done, bf16[384,8192]{1,0:T(8,128)(2,1)} %all-gather.11.cloned.1.call-done, f32[8192]{0:T(1024)S(1)} %copy-done.7, f32[384]{0:T(512)S(1)} %add_rsqrt_fusion.2), kind=kOutput, calls=%fused_computation.28 | convolution fusion | flops 4844716032 | bytes 19498496 | tf_op jit(solution)/shard_map/td,dmc->tmc/dot_general | solution.py:42
  521.0 0.7 fusion.60
  522.0 0.8 multiply_convert_fusion
  522.9 0.5 all-gather.15.cloned.1.call-update
  523.4 0.7 iota_compare_fusion
  524.3 52.7 %all-gather.17.cloned.1.call-done = bf16[3072,2,128]{2,0,1:T(8,128)(2,1)} async-done(((bf16[384,2,128]{2,0,1:T(8,128)(2,1)}), bf16[3072,2,128]{2,0,1:T(8,128)(2,1)}) %all-gather.17.cloned.1.call-update) | async-done | bytes 1572880 | tf_op jit(solution)/shard_map/all_gather | solution.py:89
  577.0 7.9 %fusion.6 = (f32[2,384]{1,0:T(2,128)S(1)}, f32[2,384,3072]{2,1,0:T(8,128)}) fusion(pred[384,3072]{1,0:T(8,128)(4,1)S(1)} %iota_compare_fusion, bf16[3072,2,128]{2,0,1:T(8,128)(2,1)} %all-gather.17.cloned.1.call-done, f32[384,2,128]{2,0,1:T(8,128)S(1)} %copy.42, f32[384,2]{0,1:T(2,128)S(1)} %add_rsqrt_fusion.1), kind=kOutput, calls=%fused_computation.11 | convolution fusion | flops 611253504 | bytes 12589056 | tf_op jit(solution)/shard_map/thd,shd->hts/dot_general | solution.py:92
  584.9 47.2 %all-gather.15.cloned.1.call-done = bf16[3072,2,128]{0,2,1:T(8,128)(2,1)} async-done(((bf16[384,2,128]{0,2,1:T(8,128)(2,1)}), bf16[3072,2,128]{0,2,1:T(8,128)(2,1)}) %all-gather.15.cloned.1.call-update) | async-done | bytes 1572880 | tf_op jit(solution)/shard_map/all_gather | solution.py:90
  632.1 6.4 fusion.36
  638.5 0.8 copy.44
  (54 shorter events, 3.3 us)
Async XLA Ops:
  7.2 1.0 copy-start
  7.2 232.9 %copy-start.6 = (f32[8192]{0:T(1024)S(1)}, f32[8192]{0:T(1024)}, u32[]{:S(2)}) copy-start(f32[8192]{0:T(1024)} %param.10) | copy-start | bytes 98308
  7.2 86.4 %all-gather.7.cloned.1.call-start = ((), (), s32[]{:S(2)}) async-start(), calls=%async_computation | async-start | bytes 6488064 | tf_op jit(solution)/shard_map/all_gather | solution.py:62
  9.8 230.2 %all-gather.9.cloned.1.call-start = ((), (), s32[]{:S(2)}) async-start(), calls=%async_computation.1 | async-start | bytes 14155776 | tf_op jit(solution)/shard_map/all_gather | solution.py:65
  10.6 352.5 %all-gather.11.cloned.1.call-start = ((), (), s32[]{:S(2)}) async-start(), calls=%async_computation.2 | async-start | bytes 6488064 | tf_op jit(solution)/shard_map/all_gather | solution.py:79
  97.7 154.6 %copy-start.5 = (f32[3,3,256]{2,1,0:T(4,128)S(1)}, f32[3,3,256]{2,1,0:T(4,128)}, u32[]{:S(2)}) copy-start(f32[3,3,256]{2,1,0:T(4,128)} %param.12) | copy-start | bytes 27652
  251.0 6.8 %copy-start.8 = (pred[8,49]{0,1:T(8,128)(4,1)S(1)}, pred[8,49]{0,1:T(8,128)(4,1)}, u32[]{:S(2)}) copy-start(pred[8,49]{0,1:T(8,128)(4,1)} %constant.31) | copy-start | bytes 1180
  251.0 5.5 collective-permute-start
  258.1 4.9 copy-start.4
  261.6 6.2 collective-permute-start.1
  268.7 4.3 copy-start.3
  268.7 5.1 copy-start.2
  273.0 236.4 %copy-start.7 = (f32[8192]{0:T(1024)S(1)}, f32[8192]{0:T(1024)}, u32[]{:S(2)}) copy-start(f32[8192]{0:T(1024)} %param.14) | copy-start | bytes 98308
  273.8 235.6 %all-gather.13.cloned.1.call-start = ((), (), s32[]{:S(2)}) async-start(), calls=%async_computation.3 | async-start | bytes 14155776 | tf_op jit(solution)/shard_map/all_gather | solution.py:81
  275.6 301.4 %all-gather.17.cloned.1.call-start = ((), (), s32[]{:S(2)}) async-start(), calls=%async_computation.5 | async-start | bytes 1769472 | tf_op jit(solution)/shard_map/all_gather | solution.py:89
  522.8 109.3 %all-gather.15.cloned.1.call-start = ((), (), s32[]{:S(2)}) async-start(), calls=%async_computation.4 | async-start | bytes 1769472 | tf_op jit(solution)/shard_map/all_gather | solution.py:90
  632.1 7.2 %copy-start.1 = (bf16[512,256]{1,0:T(8,128)(2,1)S(1)}, bf16[512,256]{1,0:T(8,128)(2,1)}, u32[]{:S(2)}) copy-start(bf16[512,256]{1,0:T(8,128)(2,1)} %param.9) | copy-start | bytes 786436
Sparse Core Ops, SparseCore 0:
  10.4 83.1 all-gather.6
  96.2 143.7 all-gather.8
  273.9 89.1 all-gather.10
  365.5 143.7 all-gather.12
  523.0 53.9 all-gather.16
  579.9 52.1 all-gather.14
where the time goes:
time: 652 us; the launch traced here: 646 us
  waiting for transfers between devices  564 us (87%)
  matrix products  43.1 us (7%)
  between operations  14.5 us (2%)
  other arithmetic  11.3 us (2%)
  local copies, waits for them, and re-layouts  10.2 us (2%)
    all_gather x1, waiting for transfers between devices, local(): lax.all_gather(hyena_weight, 'ctx', axis=0, tiled=True)  142 us
    all_gather x1, waiting for transfers between devices, local(): lax.all_gather(attn_weight, 'ctx', axis=0, tiled=True)  142 us
    all_gather x1, waiting for transfers between devices, local(): stream_whole = lax.all_gather(mixed, 'fsdp', axis=1, tiled=True)  87.2 us
    all_gather x1, waiting for transfers between devices, local(): whole_rows = lax.all_gather(features, 'fsdp', axis=1, tiled=True)  83 us
    all_gather x1, waiting for transfers between devices, local(): key_block = lax.all_gather(unit_k, 'ctx', axis=0, tiled=True)  52.7 us
    all_gather x1, waiting for transfers between devices, local(): value_block = lax.all_gather(values_in, 'ctx', axis=0, tiled=True)  47.2 us
    dot_general x2, matrix products, add_rows(): jnp.einsum('td,dmc->tmc', columns, segment, preferred_element_type=jnp.fl...  22.6 us
  transfers between devices with their start and end apart: 8, of which 8 were waited for; matrix products, arithmetic and copies ran while one was open for 3% of the time, Pallas kernels for 0%

commit v1 on v0

v1 whole, which is shorter than its diff:
```python
import functools

import jax
import jax.numpy as jnp
from jax import lax
from jax.experimental import pallas as pl
from jax.experimental.pallas import tpu as pltpu
from jax.sharding import PartitionSpec as P

MESH = pl.DeviceIdType.MESH
F32, BF16 = jnp.float32, jnp.bfloat16
T = 384
V = 512
C = 256
KD = 1024
D = 8192
HEAD = 128
LONG = 128
EPS = 1e-6
HALF = T // 2


def dot(a, b):
    return jnp.dot(a, b, preferred_element_type=F32)


def split_pair(values):
    high = values.astype(BF16)
    low = (values - high.astype(F32)).astype(BF16)
    lanes = lax.broadcasted_iota(jnp.int32, (values.shape[0], 128), 1)
    wide = jnp.where(lanes < 64, high.astype(F32), low.astype(F32))
    return wide.astype(BF16)


def join_pair(wide):
    wide = wide.astype(F32)
    return wide[:, 0:1] + wide[:, 64:65]


def kernel(
    ids, emb, g1, w1, sf, lf, g2, w2,
    mixed_out, att_out,
    idbuf, ebuf, xbuf, pbuf, rsbuf, tbuf, sbuf, prbuf, ext, lcbuf, mbuf,
    w2all, mall, pp, ssb, gs, gr, qbuf, kvall, oloc, obuf,
    id_s, id_r, sc_s, sc_r, az_s, az_r, ax_s, ax_r, ac_s, ac_r,
    rs_s, rs_r, ag_s, ag_r, w_s, w_r, e1_s, e1_r, zr_s, zr_r, zl_s, zl_r, sib_s, sib_r,
    g_s, g_r, kv_s, kv_r, o_s, o_r,
):
    c = lax.axis_index("ctx")
    f = lax.axis_index("fsdp")
    xh, y = c // 4, c % 4
    xl, z, k = f // 16, (f // 2) % 8, f % 2

    def dev(xh_, y_, xl_, z_, k_):
        return (xh_ * 4 + y_, xl_ * 16 + z_ * 2 + k_)

    def ctx_peer(d):
        return ((c + d) % 8, f)

    def z_peer(d):
        return dev(xh, y, xl, (z + d) % 8, k)

    def y_peer(d):
        return dev(xh, (y + d) % 4, xl, z, k)

    x_sib = dev(xh, y, 1 - xl, z, k)
    core_sib = dev(xh, y, xl, z, 1 - k)
    x_far = dev(1 - xh, y, xl, z, k)

    def remote(src, dst, ss, rs, to):
        return pltpu.make_async_remote_copy(
            src_ref=src, dst_ref=dst, send_sem=ss, recv_sem=rs, device_id=to, device_id_type=MESH
        )

    barrier = pltpu.get_barrier_semaphore()
    count = 0
    peers = [ctx_peer(d) for d in range(1, 8)] + [z_peer(d) for d in range(1, 8)] + [x_sib, core_sib]
    peers += [dev(xl, z // 2, xh, 2 * y + e, k) for e in range(2)]
    peers += [dev(xl, y, a, z, k) for a in range(2)]
    peers += [dev(a, y, xh, z, k) for a in range(2)]
    for p in peers:
        pl.semaphore_signal(barrier, inc=1, device_id=p, device_id_type=MESH)
        count += 1
    pl.semaphore_wait(barrier, count)

    def id_copy():
        return remote(ids, idbuf, id_s, id_r, ctx_peer(1))

    @pl.when(c < 7)
    def _():
        id_copy().start()

    rows_of = lambda xl_, z_: pl.ds(pl.multiple_of(xl_ * 256 + z_ * 32, 32), 32)

    def sc_copy(e):
        rows = rows_of(xh, 2 * y + e)
        cols = pl.ds(pl.multiple_of((z % 2) * C, C), C)
        src, dst = emb.at[rows, :], ebuf.at[k, rows, cols]
        return src, dst, remote(src, dst, sc_s.at[e], sc_r.at[z % 2], dev(xl, z // 2, xh, 2 * y + e, k))

    for e in range(2):
        src, dst, cp = sc_copy(e)
        me = (xl == xh) & (z // 2 == y) & (2 * y + e == z)

        @pl.when(me)
        def _():
            pltpu.make_async_copy(src, dst, sc_r.at[z % 2]).start()

        @pl.when(jnp.logical_not(me))
        def _():
            cp.start()

    def w_copy(d):
        slot = {1: 0, -1: 1}[d]
        return remote(w2, w2all.at[y], w_s.at[slot], w_r.at[slot], y_peer(d))

    def w_forward(d):
        slot = {1: 2, -1: 3}[d]
        half = {1: 0, -1: 1}[d]
        part = w2all.at[(y - d) % 4, :, pl.ds(half * (KD // 2), KD // 2), :]
        return remote(part, part, w_s.at[slot], w_r.at[slot], y_peer(d))

    w_copy(1).start()
    w_copy(-1).start()
    w_local = pltpu.make_async_copy(w2, w2all.at[y], w_s.at[4])
    w_local.start()

    for zb in range(2):
        rows = rows_of(xl, z)
        piece = ebuf.at[k, rows, pl.ds(zb * C, C)]
        remote(piece, piece, sc_s.at[zb], sc_r.at[zb], core_sib).wait_recv()

    def az_copy(d):
        piece = ebuf.at[k, rows_of(xl, z), :]
        return remote(piece, piece, az_s.at[d], az_r.at[d], z_peer(d))

    def ax_copy(d):
        piece = ebuf.at[k, rows_of(xl, (z - d) % 8), :]
        return remote(piece, piece, ax_s.at[d], ax_r.at[d], x_sib)

    def ac_copy(d, s):
        xl_ = (xl + s) % 2
        piece = ebuf.at[k, rows_of(xl_, (z - d) % 8), :]
        return remote(piece, piece, ac_s.at[s, d], ac_r.at[s, d], core_sib)

    order = (1, 7, 2, 6, 3, 5, 4)
    for d in order:
        az_copy(d).start()
    ax_copy(0).start()
    ac_copy(0, 0).start()
    for d in order:
        az_copy(d).wait_recv()
        ax_copy(d).start()
        ac_copy(d, 0).start()
    for d in (0,) + order:
        ax_copy(d).wait_recv()
        ac_copy(d, 1).start()
    for d in (0,) + order:
        ac_copy(d, 0).wait_recv()
        ac_copy(d, 1).wait_recv()

    gain = g1[pl.ds(c, 1), :]
    squares = jnp.zeros((V, 1), F32)
    for q in range(4):
        e = ebuf[q % 2, :, (q // 2) * C : (q // 2 + 1) * C].astype(F32)
        squares = squares + jnp.sum(e * e, axis=1, keepdims=True)
        xbuf[:, q * C : (q + 1) * C] = (e * gain[:, q * C : (q + 1) * C]).astype(BF16)
    pbuf[:, 3 * C : 3 * C + 128] = split_pair(squares)
    for m in range(3):
        pbuf[:, m * C : (m + 1) * C] = dot(xbuf[...], w1[m]).astype(BF16)

    def rs_copy(d):
        rows = pl.ds(pl.multiple_of(((c + d) % 8) * 64, 64), 64)
        return remote(pbuf.at[rows, :], rsbuf.at[d - 1], rs_s.at[d - 1], rs_r.at[d - 1], ctx_peer(d))

    def ag_copy(d):
        rows = pl.ds(pl.multiple_of(c * 64, 64), 64)
        return remote(tbuf.at[rows, :], tbuf.at[rows, :], ag_s.at[d - 1], ag_r.at[d - 1], ctx_peer(d))

    for d in range(1, 8):
        rs_copy(d).start()
    mine = pl.ds(pl.multiple_of(c * 64, 64), 64)
    total = pbuf[mine, : 3 * C].astype(F32)
    sq = join_pair(pbuf[mine, 3 * C :])
    for d in range(1, 8):
        rs_copy(d).wait_recv()
        total = total + rsbuf[d - 1, :, : 3 * C].astype(F32)
        sq = sq + join_pair(rsbuf[d - 1, :, 3 * C :])
    tbuf[mine, :] = (total * lax.rsqrt(sq / D + EPS)).astype(BF16)
    for d in range(1, 8):
        ag_copy(d).start()

    @pl.when(c > 0)
    def _():
        id_copy().wait_recv()

    @pl.when(c == 0)
    def _():
        idbuf[...] = jnp.full(idbuf.shape, -1, jnp.int32)

    for d in range(1, 8):
        ag_copy(d).wait_recv()

    w_copy(1).wait_recv()
    w_forward(1).start()
    w_copy(-1).wait_recv()
    w_forward(-1).start()

    def one_hot(chunk):
        row = idbuf[:, 128 + chunk * 128 : 256 + chunk * 128] if chunk < 2 else ids[:, (chunk - 2) * 128 : (chunk - 1) * 128]
        words = lax.broadcasted_iota(jnp.int32, (V, 128), 0)
        return jnp.where(words == row, 1.0, 0.0).astype(BF16)

    def pick(hot, values):
        return lax.dot_general(hot, values, (((0,), (0,)), ((), ())), preferred_element_type=F32)

    for chunk in range(5):
        sbuf[chunk * 128 : (chunk + 1) * 128, :] = pick(one_hot(chunk), tbuf[...])

    def short(m, start, size):
        cols = slice(m * C, (m + 1) * C)
        out = sf[m : m + 1, :] * sbuf[start : start + size, cols]
        for j in range(1, 3):
            out = out + sf[3 * j + m : 3 * j + m + 1, :] * sbuf[start - j : start - j + size, cols]
        return out

    for chunk in range(4):
        prod = (short(1, 128 + chunk * 128, 128) * short(2, 128 + chunk * 128, 128)).astype(BF16).astype(F32)
        for lt in range(2):
            prbuf[lt, chunk * 128 : (chunk + 1) * 128, :] = prod[:, lt * 128 : (lt + 1) * 128]

    LANE_T = T // 8
    for lt in range(2):

        @pl.loop(0, LANE_T + LONG - 1)
        def _(i):
            ext[lt, i] = prbuf[lt, pl.ds(i + 1, 8, stride=LANE_T), :]

    for lt in range(2):
        for ig in range(3):

            def taps(j8, acc):
                window = ext[lt, pl.ds(ig * 16 + 120 - 8 * j8, 23)]
                coef = lf[pl.ds(pl.multiple_of(8 * j8, 8), 8), lt * 128 : (lt + 1) * 128]
                for jj in range(8):
                    acc = acc + coef[jj : jj + 1, :][None] * window[7 - jj : 23 - jj]
                return acc

            acc = lax.fori_loop(0, LONG // 8, taps, jnp.zeros((16, 8, 128), F32))
            for ii in range(16):
                lcbuf[lt, pl.ds(ig * 16 + ii, 8, stride=LANE_T), :] = acc[ii]

    for chunk in range(3):
        rows = slice(chunk * 128, (chunk + 1) * 128)
        features = pick(one_hot(chunk + 2), emb[...])
        gate = short(0, 256 + chunk * 128, 128)
        for lt in range(2):
            cols = slice(lt * 128, (lt + 1) * 128)
            mixed = (features[:, cols] + gate[:, cols] * lcbuf[lt, rows, :]).astype(BF16)
            mbuf[rows, cols] = mixed
            mixed_out[rows, cols] = mixed

    def cols_of(z_, k_):
        return pl.ds(pl.multiple_of((z_ * 2 + k_) * C, C), C)

    def e1_copy(a):
        dst = mall.at[xh, :, cols_of(z, k)]
        return dst, remote(mbuf, dst, e1_s.at[a], e1_r.at[xh], dev(xl, y, a, z, k))

    for a in range(2):
        dst, cp = e1_copy(a)
        me = (xl == xh) & (xl == a)

        @pl.when(me)
        def _():
            pltpu.make_async_copy(mbuf, dst, e1_r.at[xh]).start()

        @pl.when(jnp.logical_not(me))
        def _():
            cp.start()

    def chunk_of(b, z_, k_, h):
        return mall.at[b, h * HALF : (h + 1) * HALF, cols_of(z_, k_)]

    def zr_copy(b, s, h):
        piece = chunk_of(b, (z - s) % 8, k, h)
        return remote(piece, piece, zr_s.at[b, s, h], zr_r.at[b, s, h], z_peer(1))

    def zl_copy(b, s, h):
        piece = chunk_of(b, (z + s) % 8, k, h)
        return remote(piece, piece, zl_s.at[b, s, h], zl_r.at[b, s, h], z_peer(-1))

    def sib_copy(b, s, h):
        piece = chunk_of(b, (z + s) % 8, k, h)
        return remote(piece, piece, sib_s.at[b, s, h], sib_r.at[b, s, h], core_sib)

    def ring(b):
        piece = mall.at[b, :, cols_of(z, k)]
        remote(piece, piece, e1_s.at[0], e1_r.at[b], core_sib).wait_recv()
        for h in range(2):
            zr_copy(b, 0, h).start()
            zl_copy(b, 0, h).start()
        for h in range(2):
            sib_copy(b, 0, h).start()
        for s in range(1, 5):
            for h in range(2):
                if s < 4 or h == 0:
                    zr_copy(b, s - 1, h).wait_recv()
                    if s < 3 or (s == 3 and h == 0):
                        zr_copy(b, s, h).start()
                    sib_copy(b, 8 - s, h).start()
                if s < 4 or h == 1:
                    zl_copy(b, s - 1, h).wait_recv()
                    if s < 3 or (s == 3 and h == 1):
                        zl_copy(b, s, h).start()
                    sib_copy(b, s, h).start()

    def ring_end(b):
        for s in range(8):
            for h in range(2):
                sib_copy(b, s, h).wait_recv()

    ring(0)
    ring(1)
    ring_end(0)
    ring_end(1)
    w_local.wait()
    w_forward(1).wait_recv()
    w_forward(-1).wait_recv()

    def project(b):
        pp[b] = jnp.zeros(pp.shape[1:], F32)
        ssb[b] = jnp.zeros(ssb.shape[1:], F32)

        @pl.loop(0, 4)
        def _(ys):
            scale = g2[pl.ds(4 * xh + ys, 1), :]
            cols = pl.ds(pl.multiple_of(ys * KD, KD), KD)
            for r in range(3):
                rows = slice(r * 128, (r + 1) * 128)
                part = mall[b, rows, cols].astype(F32)
                ssb[b, rows, :] += jnp.sum(part * part, axis=1, keepdims=True)
                xbuf[rows, :] = (part * scale).astype(BF16)
            for m in range(3):
                pp[b, :, m * C : (m + 1) * C] += dot(xbuf[:T, :], w2all[ys, m])

    def g_copy(b):
        return remote(gs.at[b], gr.at[b], g_s.at[b], g_r.at[b], x_far)

    def head_cols(m, h):
        return pl.ds(pl.multiple_of(m * C + h * HEAD, HEAD), HEAD)

    def send_half(b):
        for m in range(3):
            gs[b, m] = pp[b, :, head_cols(m, 1 - xh)].astype(BF16)
        gs[b, 3] = split_pair(ssb[b, :, 0:1])
        g_copy(b).start()

    def head_norm(values):
        values = values.astype(F32)
        return (values * lax.rsqrt(jnp.mean(values * values, axis=1, keepdims=True) + EPS)).astype(BF16)

    def kv_copy(b, d):
        block = kvall.at[y, b]
        return remote(block, block, kv_s.at[b, d - 1], kv_r.at[b, d - 1], y_peer(d))

    def finish(b):
        g_copy(b).wait_recv()
        row = lax.rsqrt((ssb[b, :, 0:1] + join_pair(gr[b, 3])) / D + EPS)
        triple = [((pp[b, :, head_cols(m, xh)] + gr[b, m].astype(F32)) * row).astype(BF16) for m in range(3)]
        kvall[y, b, 0] = head_norm(triple[1])
        kvall[y, b, 1] = triple[2]
        for d in range(1, 4):
            kv_copy(b, d).start()
        qbuf[b] = head_norm(triple[0])

    project(0)
    send_half(0)
    project(1)
    send_half(1)
    finish(0)
    finish(1)
    for b in range(2):
        for d in range(1, 4):
            kv_copy(b, d).wait_recv()

    factor = 2.0 * HEAD ** -0.5

    def attend(b):
        @pl.loop(0, 3)
        def _(qc):
            rows = pl.ds(pl.multiple_of(qc * 128, 128), 128)
            query = qbuf[b, rows, :]

            def weights(ys, kb):
                score = lax.dot_general(
                    query, kvall[ys, kb, 0], (((1,), (1,)), ((), ())), preferred_element_type=F32
                )
                return jnp.exp(score * factor)

            def add(carry, weight, ys, kb):
                num, den = carry
                den = den + jnp.sum(weight, axis=1, keepdims=True)
                return num + dot(weight.astype(BF16), kvall[ys, kb, 1]), den

            def full(kb):
                return lambda ys, carry: add(carry, weights(ys, kb), ys, kb)

            carry = (jnp.zeros((128, HEAD), F32), jnp.zeros((128, 1), F32))
            if b == 1:
                carry = lax.fori_loop(0, 4, full(0), carry)
            carry = lax.fori_loop(0, y, full(b), carry)
            weight = weights(y, b)
            at = qc * 128 + lax.broadcasted_iota(jnp.int32, (128, T), 0)
            key = lax.broadcasted_iota(jnp.int32, (128, T), 1)
            weight = jnp.where(key <= at, weight, 0.0)
            num, den = add(carry, weight, y, b)
            oloc[b, rows, :] = (num / den).astype(BF16)

    attend(0)
    attend(1)

    here = pl.ds(pl.multiple_of(xh * HEAD, HEAD), HEAD)
    there = pl.ds(pl.multiple_of((1 - xh) * HEAD, HEAD), HEAD)
    o_copy = remote(oloc.at[1 - xh], obuf, o_s, o_r, x_far)
    o_copy.start()
    att_out[:, here] = oloc[xh]
    o_copy.wait_recv()
    att_out[:, there] = obuf[...]

    @pl.when(c < 7)
    def _():
        id_copy().wait_send()

    for e in range(2):
        me = (xl == xh) & (z // 2 == y) & (2 * y + e == z)

        @pl.when(jnp.logical_not(me))
        def _():
            sc_copy(e)[2].wait_send()

    for a in range(2):
        me = (xl == xh) & (xl == a)

        @pl.when(jnp.logical_not(me))
        def _():
            e1_copy(a)[1].wait_send()

    for d in (1, -1):
        w_copy(d).wait_send()
        w_forward(d).wait_send()
    for d in order:
        az_copy(d).wait_send()
    for d in range(8):
        ax_copy(d).wait_send()
        ac_copy(d, 0).wait_send()
        ac_copy(d, 1).wait_send()
    for d in range(1, 8):
        rs_copy(d).wait_send()
        ag_copy(d).wait_send()
    for b in range(2):
        for s in range(4):
            for h in range(2):
                if s < 3 or h == 0:
                    zr_copy(b, s, h).wait_send()
                if s < 3 or h == 1:
                    zl_copy(b, s, h).wait_send()
        for s in range(8):
            for h in range(2):
                sib_copy(b, s, h).wait_send()
        g_copy(b).wait_send()
        for d in range(1, 4):
            kv_copy(b, d).wait_send()
    o_copy.wait_send()


def local(base_ids, embedding, first_gain, hyena_weight, short_filter, long_filter, second_gain, attn_weight):
    dma = pltpu.SemaphoreType.DMA
    vmem = pltpu.VMEM
    scratch = [
        vmem((1, T), jnp.int32),
        vmem((2, V, 2 * C), BF16),
        vmem((V, KD), BF16),
        vmem((V, 3 * C + 128), BF16),
        vmem((7, 64, 3 * C + 128), BF16),
        vmem((V, 3 * C), BF16),
        vmem((640, 3 * C), F32),
        vmem((2, 512, 128), F32),
        vmem((2, T // 8 + LONG, 8, 128), F32),
        vmem((2, T, 128), F32),
        vmem((T, C), BF16),
        vmem((4, 3, KD, C), BF16),
        vmem((2, T, 16 * C), BF16),
        vmem((2, T, 3 * C), F32),
        vmem((2, T, 128), F32),
        vmem((2, 4, T, HEAD), BF16),
        vmem((2, 4, T, HEAD), BF16),
        vmem((2, T, HEAD), BF16),
        vmem((4, 2, 2, T, HEAD), BF16),
        vmem((2, T, HEAD), BF16),
        vmem((T, HEAD), BF16),
        dma, dma,
        dma((2,)), dma((2,)),
        dma((8,)), dma((8,)),
        dma((8,)), dma((8,)),
        dma((2, 8)), dma((2, 8)),
        dma((7,)), dma((7,)),
        dma((7,)), dma((7,)),
        dma((5,)), dma((4,)),
        dma((2,)), dma((2,)),
        dma((2, 4, 2)), dma((2, 4, 2)),
        dma((2, 4, 2)), dma((2, 4, 2)),
        dma((2, 8, 2)), dma((2, 8, 2)),
        dma((2,)), dma((2,)),
        dma((2, 3)), dma((2, 3)),
        dma, dma,
    ]
    return pl.pallas_call(
        kernel,
        out_shape=(jax.ShapeDtypeStruct((T, C), BF16), jax.ShapeDtypeStruct((T, C), BF16)),
        in_specs=[pl.BlockSpec(memory_space=pltpu.VMEM)] * 8,
        out_specs=(pl.BlockSpec(memory_space=pltpu.VMEM), pl.BlockSpec(memory_space=pltpu.VMEM)),
        scratch_shapes=scratch,
        compiler_params=pltpu.CompilerParams(
            collective_id=0, has_side_effects=True, vmem_limit_bytes=56 << 20
        ),
    )(
        base_ids.reshape(1, T),
        embedding,
        first_gain.reshape(8, KD),
        jnp.transpose(hyena_weight, (1, 0, 2)),
        short_filter.reshape(9, C),
        long_filter,
        second_gain.reshape(8, KD),
        jnp.transpose(attn_weight, (1, 0, 2)),
    )


def solution(mesh):
    return jax.shard_map(
        local,
        mesh=mesh,
        in_specs=(
            P("ctx"),
            P(None, "fsdp"),
            P(),
            P("ctx", None, "fsdp"),
            P(None, None, "fsdp"),
            P(None, "fsdp"),
            P(),
            P("ctx", None, "fsdp"),
        ),
        out_specs=(P("ctx", "fsdp"), P("ctx", "fsdp")),
        check_vma=False,
    )
```

time: 652 us -> 183 us (0.28)
  waiting for transfers between devices: 564 us -> 0 us
  Pallas kernels: 0 us -> 172 us
  matrix products: 43.1 us -> 0 us
  between operations: 14.5 us -> 0.64 us
  other arithmetic: 11.3 us -> 0 us
    all_gather x6 -> x0, waiting for transfers between devices: 555 us -> none  [the longest x1 142 us: local(): lax.all_gather(hyena_weight, 'ctx', axis=0, tiled=True)]
    pallas_call x0 -> x1, Pallas kernels: none -> 172 us  [local(): pl.pallas_call(kernel, out_shape=(jax.ShapeDtypeStruct((T, C), BF16), jax...]
    dot_general x5 -> x0, matrix products: 38.5 us -> none  [the longest x2 22.6 us: add_rows(): jnp.einsum('td,dmc->tmc', columns, segment, preferred_element_type=jnp.fl...]
    reduce_sum x4 -> x0, other arithmetic: 8.32 us -> none  [the longest x2 8.21 us: norm_rows(): jnp.mean(values * values, axis=-1, keepdims=True) + 1e-06]
    ppermute x2 -> x0, waiting for transfers between devices: 8.25 us -> none  [shifted(): return lax.ppermute(shard, axis, pairs)]
  transfers between devices with their start and end apart: 8 -> 0, of which waited for: 8 -> 0; matrix products, arithmetic and copies ran while one was open for 3% -> 0% of each run, Pallas kernels for 0% -> 0%
where the time goes in v1:
time: 183 us; the launch traced here: 181 us
  Pallas kernels  172 us (94%)
  local copies, waits for them, and re-layouts  8.59 us (5%)
    pallas_call x1, Pallas kernels, local(): pl.pallas_call(kernel, out_shape=(jax.ShapeDtypeStruct((T, C), BF16), jax...  172 us

profile of v1, /device:TPU:28, one launch (start us, length us, event | category | flops | bytes accessed | tf_op | source)
XLA Modules:
  0.0 180.8 jit_solution(17168579374474829719)
XLA Ops:
  0.6 1.3 reshape.16.ids
  1.9 1.3 reshape.18.sf
  3.2 1.4 reshape.17.g1
  4.6 1.4 reshape.19.g2
  6.0 171.6 %shard_map.95 = (bf16[384,256]{1,0:T(8,128)(2,1)}, bf16[384,256]{1,0:T(8,128)(2,1)}) custom-call(s32[1,384]{1,0:T(1,128)} %reshape.16.ids, bf16[512,256]{1,0:T(8,128)(2,1)} %emb.1, f32[8,1024]{1,0:T(8,128)} %reshape.17.g1, bf16[3,1024,256]{2,1,0:T(8,128)(2,1)} %bitcast.2, f32[9,256]{1,0:T(8,128)} %reshape.18.sf, f32[128,256]{1,0:T(8,128)} %lf.1, ...), custom_call_target="tpu_custom_call" | custom-call | tf_op jit(solution)/shard_map/pallas_call | solution.py:518
  177.6 1.6 copy.12
  179.2 1.6 copy.13

commit v2 on v1

v2 whole, which is shorter than its diff:
```python
import functools

import jax
import jax.numpy as jnp
from jax import lax
from jax.experimental import pallas as pl
from jax.experimental.pallas import tpu as pltpu
from jax.sharding import PartitionSpec as P

MESH = pl.DeviceIdType.MESH
F32, BF16 = jnp.float32, jnp.bfloat16
T = 384
V = 512
C = 256
KD = 1024
D = 8192
HEAD = 128
LONG = 128
EPS = 1e-6


def dot(a, b):
    return jnp.dot(a, b, preferred_element_type=F32)


def kernel(
    ids, emb, g1, w1, sf, lf, g2, w2,
    mixed_out, att_out,
    idbuf, ebuf, xbuf, pkv, pq, psq, rskv, rsq, rssq, tkv, tq, sbuf, prbuf, ext, lcbuf, mbuf,
    w2all, mall, xs, pp, ssb, gs, gr, sqs, sqr, qbuf, kvall, oloc, obuf,
    id_s, id_r, sc_s, sc_r, az_s, az_r, ax_s, ax_r, ac_s, ac_r,
    rs_s, rs_r, ag_s, ag_r, w_s, w_r, wl_s, e1_s, e1_r, zr_s, zr_r, zl_s, zl_r, sib_s, sib_r,
    g_s, g_r, kv_s, kv_r, o_s, o_r,
):
    c = lax.axis_index("ctx")
    f = lax.axis_index("fsdp")
    xh, y = c // 4, c % 4
    xl, z, k = f // 16, (f // 2) % 8, f % 2

    def dev(xh_, y_, xl_, z_, k_):
        return (xh_ * 4 + y_, xl_ * 16 + z_ * 2 + k_)

    def ctx_peer(d):
        return ((c + d) % 8, f)

    def z_peer(d):
        return dev(xh, y, xl, (z + d) % 8, k)

    def y_peer(d):
        return dev(xh, (y + d) % 4, xl, z, k)

    x_sib = dev(xh, y, 1 - xl, z, k)
    core_sib = dev(xh, y, xl, z, 1 - k)
    x_far = dev(1 - xh, y, xl, z, k)

    def remote(src, dst, ss, rs, to):
        return pltpu.make_async_remote_copy(
            src_ref=src, dst_ref=dst, send_sem=ss, recv_sem=rs, device_id=to, device_id_type=MESH
        )

    barrier = pltpu.get_barrier_semaphore()
    count = 0
    peers = [ctx_peer(d) for d in range(1, 8)] + [z_peer(d) for d in range(1, 8)] + [x_sib, core_sib]
    peers += [dev(xl, z // 2, xh, 2 * y + e, k) for e in range(2)]
    peers += [dev(xl, y, a, z, k) for a in range(2)]
    peers += [dev(a, y, xh, z, k) for a in range(2)]
    for p in peers:
        pl.semaphore_signal(barrier, inc=1, device_id=p, device_id_type=MESH)
        count += 1
    pl.semaphore_wait(barrier, count)

    def id_copy():
        return remote(ids, idbuf, id_s, id_r, ctx_peer(1))

    @pl.when(c < 7)
    def _():
        id_copy().start()

    rows_of = lambda xl_, z_: pl.ds(pl.multiple_of(xl_ * 256 + z_ * 32, 32), 32)

    def sc_copy(e):
        rows = rows_of(xh, 2 * y + e)
        cols = pl.ds(pl.multiple_of((z % 2) * C, C), C)
        src, dst = emb.at[rows, :], ebuf.at[k, rows, cols]
        return src, dst, remote(src, dst, sc_s.at[e], sc_r.at[z % 2], dev(xl, z // 2, xh, 2 * y + e, k))

    for e in range(2):
        src, dst, cp = sc_copy(e)
        me = (xl == xh) & (z // 2 == y) & (2 * y + e == z)

        @pl.when(me)
        def _():
            pltpu.make_async_copy(src, dst, sc_r.at[z % 2]).start()

        @pl.when(jnp.logical_not(me))
        def _():
            cp.start()

    W_PARTS = ((1, 3, 0, KD // 2), (1, 3, KD // 2, KD // 2), (0, 1, 0, KD))

    def w_copy(part, d):
        m0, m1, row, count_ = W_PARTS[part]
        side = {1: 0, -1: 1}[d]
        cut = (slice(m0, m1), slice(row, row + count_), slice(None))
        return remote(
            w2.at[cut], w2all.at[(y,) + cut], w_s.at[part, 0, side], w_r.at[part, 0, side], y_peer(d)
        )

    def w_forward(part, d):
        m0, m1, row, count_ = W_PARTS[part]
        side = {1: 0, -1: 1}[d]
        half = count_ // 2
        piece = w2all.at[(y - d) % 4, m0:m1, row + side * half : row + (side + 1) * half, :]
        return remote(piece, piece, w_s.at[part, 1, side], w_r.at[part, 1, side], y_peer(d))

    def w_send(part):
        for d in (1, -1):
            w_copy(part, d).start()

    def w_pass(part):
        for d in (1, -1):
            w_copy(part, d).wait_recv()
            w_forward(part, d).start()

    def w_land(part):
        for d in (1, -1):
            w_forward(part, d).wait_recv()

    w_local = pltpu.make_async_copy(w2, w2all.at[y], wl_s)
    w_local.start()
    w_send(0)

    for zb in range(2):
        rows = rows_of(xl, z)
        piece = ebuf.at[k, rows, pl.ds(zb * C, C)]
        remote(piece, piece, sc_s.at[zb], sc_r.at[zb], core_sib).wait_recv()

    def az_copy(d):
        piece = ebuf.at[k, rows_of(xl, z), :]
        return remote(piece, piece, az_s.at[d], az_r.at[d], z_peer(d))

    def ax_copy(d):
        piece = ebuf.at[k, rows_of(xl, (z - d) % 8), :]
        return remote(piece, piece, ax_s.at[d], ax_r.at[d], x_sib)

    def ac_copy(d, s):
        xl_ = (xl + s) % 2
        piece = ebuf.at[k, rows_of(xl_, (z - d) % 8), :]
        return remote(piece, piece, ac_s.at[s, d], ac_r.at[s, d], core_sib)

    order = (1, 7, 2, 6, 3, 5, 4)
    for d in order:
        az_copy(d).start()
    ax_copy(0).start()
    ac_copy(0, 0).start()
    for d in order:
        az_copy(d).wait_recv()
        ax_copy(d).start()
        ac_copy(d, 0).start()
    for d in (0,) + order:
        ax_copy(d).wait_recv()
        ac_copy(d, 1).start()
    for d in (0,) + order:
        ac_copy(d, 0).wait_recv()
        ac_copy(d, 1).wait_recv()

    gain = g1[pl.ds(pl.multiple_of(c * KD, KD), KD)].reshape(1, KD)
    squares = jnp.zeros((V, 1), F32)
    for q in range(4):
        e = ebuf[q % 2, :, (q // 2) * C : (q // 2 + 1) * C].astype(F32)
        squares = squares + jnp.sum(e * e, axis=1, keepdims=True)
        xbuf[:, q * C : (q + 1) * C] = (e * gain[:, q * C : (q + 1) * C]).astype(BF16)
    psq[...] = jnp.transpose(jnp.broadcast_to(squares, (V, 128)))[0:1, :]

    mine = pl.ds(pl.multiple_of(c * 64, 64), 64)

    def rs_copy(kind, d):
        rows = pl.ds(pl.multiple_of(((c + d) % 8) * 64, 64), 64)
        src = (pkv.at[rows, :], pq.at[rows, :], psq)[kind]
        dst = (rskv, rsq, rssq)[kind].at[d - 1]
        return remote(src, dst, rs_s.at[kind, d - 1], rs_r.at[kind, d - 1], ctx_peer(d))

    def ag_copy(kind, d):
        piece = (tkv, tq)[kind].at[mine, :]
        return remote(piece, piece, ag_s.at[kind, d - 1], ag_r.at[kind, d - 1], ctx_peer(d))

    ctx_order = (4, 1, 7, 2, 6, 3, 5)
    for d in ctx_order:
        rs_copy(2, d).start()
    for m in (1, 2):
        pkv[:, (m - 1) * C : m * C] = dot(xbuf[...], w1[m]).astype(BF16)
    for d in ctx_order:
        rs_copy(0, d).start()
    pq[...] = dot(xbuf[...], w1[0]).astype(BF16)
    for d in ctx_order:
        rs_copy(1, d).start()

    sq = psq[...]
    for d in ctx_order:
        rs_copy(2, d).wait_recv()
        sq = sq + rssq[d - 1]
    row = lax.rsqrt(sq / D + EPS)
    ssb[0] = jnp.transpose(jnp.broadcast_to(row, (128, V)))
    scale_row = ssb[0, mine, :][:, 0:1]
    total = pkv[mine, :].astype(F32)
    for d in ctx_order:
        rs_copy(0, d).wait_recv()
        total = total + rskv[d - 1].astype(F32)
    tkv[mine, :] = (total * scale_row).astype(BF16)
    for d in ctx_order:
        ag_copy(0, d).start()
    total = pq[mine, :].astype(F32)
    for d in ctx_order:
        rs_copy(1, d).wait_recv()
        total = total + rsq[d - 1].astype(F32)
    tq[mine, :] = (total * scale_row).astype(BF16)
    for d in ctx_order:
        ag_copy(1, d).start()

    @pl.when(c > 0)
    def _():
        id_copy().wait_recv()

    @pl.when(c == 0)
    def _():
        idbuf[...] = jnp.full(idbuf.shape, -1, jnp.int32)

    for d in ctx_order:
        ag_copy(0, d).wait_recv()

    def one_hot(chunk):
        row = idbuf[128 + chunk * 128 : 256 + chunk * 128] if chunk < 2 else ids[(chunk - 2) * 128 : (chunk - 1) * 128]
        words = lax.broadcasted_iota(jnp.int32, (V, 128), 0)
        return jnp.where(words == row.reshape(1, 128), 1.0, 0.0).astype(BF16)

    def pick(hot, values):
        return lax.dot_general(hot, values, (((0,), (0,)), ((), ())), preferred_element_type=F32)

    for chunk in range(5):
        sbuf[chunk * 128 : (chunk + 1) * 128, C:] = pick(one_hot(chunk), tkv[...])

    def short(m, start, size, lanes=slice(0, C)):
        cols = slice(m * C + lanes.start, m * C + lanes.stop)
        out = sf[0, m : m + 1, lanes] * sbuf[start : start + size, cols]
        for j in range(1, 3):
            out = out + sf[j, m : m + 1, lanes] * sbuf[start - j : start - j + size, cols]
        return out

    for chunk in range(4):
        prod = (short(1, 128 + chunk * 128, 128) * short(2, 128 + chunk * 128, 128)).astype(BF16).astype(F32)
        for lt in range(2):
            prbuf[lt, chunk * 128 : (chunk + 1) * 128, :] = prod[:, lt * 128 : (lt + 1) * 128]

    def cols_of(z_, k_, h):
        return pl.ds(pl.multiple_of((z_ * 2 + k_) * C + h * 128, 128), 128)

    def e1_copy(a, h):
        dst = mall.at[xh, :, cols_of(z, k, h)]
        src = mbuf.at[h]
        return src, dst, remote(src, dst, e1_s.at[a, h], e1_r.at[xh, h], dev(xl, y, a, z, k))

    def e1_send(h):
        for a in range(2):
            src, dst, cp = e1_copy(a, h)
            me = (xl == xh) & (xl == a)

            @pl.when(me)
            def _():
                pltpu.make_async_copy(src, dst, e1_r.at[xh, h]).start()

            @pl.when(jnp.logical_not(me))
            def _():
                cp.start()

    LANE_T = T // 8

    def convolve(lt):
        @pl.loop(0, LANE_T + LONG - 1)
        def _(i):
            ext[i] = prbuf[lt, pl.ds(i + 1, 8, stride=LANE_T), :]

        for ig in range(3):

            def taps(j8, acc):
                window = ext[pl.ds(ig * 16 + 120 - 8 * j8, 23)]
                coef = lf[pl.ds(pl.multiple_of(8 * j8, 8), 8), lt * 128 : (lt + 1) * 128]
                for jj in range(8):
                    acc = acc + coef[jj : jj + 1, :][None] * window[7 - jj : 23 - jj]
                return acc

            acc = lax.fori_loop(0, LONG // 8, taps, jnp.zeros((16, 8, 128), F32))
            for ii in range(16):
                lcbuf[pl.ds(ig * 16 + ii, 8, stride=LANE_T), :] = acc[ii]

    def residual(lt):
        lanes = slice(lt * 128, (lt + 1) * 128)
        for chunk in range(3):
            rows = slice(chunk * 128, (chunk + 1) * 128)
            features = pick(one_hot(chunk + 2), emb[:, lanes])
            gate = short(0, 256 + chunk * 128, 128, lanes)
            mixed = (features + gate * lcbuf[rows, :]).astype(BF16)
            mbuf[lt, rows, :] = mixed
            mixed_out[rows, lanes] = mixed

    convolve(0)
    for d in ctx_order:
        ag_copy(1, d).wait_recv()
    w_pass(0)
    w_send(1)
    for chunk in range(1, 5):
        sbuf[chunk * 128 : (chunk + 1) * 128, :C] = pick(one_hot(chunk), tq[...])
    residual(0)
    e1_send(0)
    convolve(1)
    residual(1)
    e1_send(1)

    def chunk_of(b, z_, k_, h):
        return mall.at[b, :, cols_of(z_, k_, h)]

    def zr_copy(b, s, h):
        piece = chunk_of(b, (z - s) % 8, k, h)
        return remote(piece, piece, zr_s.at[b, s, h], zr_r.at[b, s, h], z_peer(1))

    def zl_copy(b, s, h):
        piece = chunk_of(b, (z + s) % 8, k, h)
        return remote(piece, piece, zl_s.at[b, s, h], zl_r.at[b, s, h], z_peer(-1))

    def sib_copy(b, s, h):
        piece = chunk_of(b, (z + s) % 8, k, h)
        return remote(piece, piece, sib_s.at[b, s, h], sib_r.at[b, s, h], core_sib)

    def ring_start(b):
        for h in range(2):
            piece = chunk_of(b, z, k, h)
            remote(piece, piece, e1_s.at[0, h], e1_r.at[b, h], core_sib).wait_recv()
            zr_copy(b, 0, h).start()
            zl_copy(b, 0, h).start()
            sib_copy(b, 0, h).start()

    def ring_step(b, s):
        for h in range(2):
            if s < 4 or h == 0:
                zr_copy(b, s - 1, h).wait_recv()
                if s < 3 or (s == 3 and h == 0):
                    zr_copy(b, s, h).start()
                sib_copy(b, 8 - s, h).start()
            if s < 4 or h == 1:
                zl_copy(b, s - 1, h).wait_recv()
                if s < 3 or (s == 3 and h == 1):
                    zl_copy(b, s, h).start()
                sib_copy(b, s, h).start()

    def ring_end(b):
        for s in range(8):
            for h in range(2):
                sib_copy(b, s, h).wait_recv()

    def scale(b, ys):
        gain2 = g2[pl.ds(pl.multiple_of((4 * xh + ys) * KD, KD), KD)].reshape(1, KD)
        cols = pl.ds(pl.multiple_of(ys * KD, KD), KD)
        for r in range(3):
            rows = slice(r * 128, (r + 1) * 128)
            part = mall[b, rows, cols].astype(F32)
            squares_ = jnp.broadcast_to(jnp.sum(part * part, axis=1, keepdims=True), (128, 128))
            ssb[b, rows, :] = squares_ if ys == 0 else ssb[b, rows, :] + squares_
            xs[b, rows, cols] = (part * gain2).astype(BF16)

    def project(b, ys, ms):
        for m in ms:
            cols = slice(m * C, (m + 1) * C)
            term = dot(xs[b, :, ys * KD : (ys + 1) * KD], w2all[ys, m])
            pp[b, :, cols] = term if ys == 0 else pp[b, :, cols] + term

    def g_copy(b, m):
        if m == 3:
            return remote(sqs.at[b], sqr.at[b], g_s.at[b, m], g_r.at[b, m], x_far)
        return remote(gs.at[b, m], gr.at[b, m], g_s.at[b, m], g_r.at[b, m], x_far)

    def head_cols(m, h):
        return pl.ds(pl.multiple_of(m * C + h * HEAD, HEAD), HEAD)

    def send_half(b, ms):
        for m in ms:
            gs[b, m] = pp[b, :, head_cols(m, 1 - xh)].astype(BF16)
            g_copy(b, m).start()

    def send_squares(b):
        sqs[b] = jnp.transpose(ssb[b, :T, :])[0:1, :]
        g_copy(b, 3).start()

    def row_factor(b):
        g_copy(b, 3).wait_recv()
        other = jnp.transpose(jnp.broadcast_to(sqr[b], (128, T)))
        ssb[b, :T, :] = lax.rsqrt((ssb[b, :T, :] + other) / D + EPS)

    def head_norm(values):
        values = values.astype(F32)
        return (values * lax.rsqrt(jnp.mean(values * values, axis=1, keepdims=True) + EPS)).astype(BF16)

    def kv_copy(b, d):
        block = kvall.at[y, b]
        return remote(block, block, kv_s.at[b, d - 1], kv_r.at[b, d - 1], y_peer(d))

    def joined(b, m):
        g_copy(b, m).wait_recv()
        return ((pp[b, :, head_cols(m, xh)] + gr[b, m].astype(F32)) * ssb[b, :T, :]).astype(BF16)

    def finish_kv(b):
        row_factor(b)
        kvall[y, b, 0] = head_norm(joined(b, 1))
        kvall[y, b, 1] = joined(b, 2)
        for d in range(1, 4):
            kv_copy(b, d).start()

    def finish_q(b):
        qbuf[b] = head_norm(joined(b, 0))

    def kv_wait(b):
        for d in range(1, 4):
            kv_copy(b, d).wait_recv()

    ring_start(0)
    ring_step(0, 1)
    w_pass(1)
    w_send(2)
    ring_step(0, 2)
    ring_step(0, 3)
    ring_start(1)
    ring_step(0, 4)
    ring_end(0)
    w_local.wait()
    w_land(0)
    w_land(1)
    scale(0, 0)
    project(0, 0, (1, 2))
    ring_step(1, 1)
    scale(0, 1)
    project(0, 1, (1, 2))
    scale(0, 2)
    project(0, 2, (1, 2))
    ring_step(1, 2)
    scale(0, 3)
    project(0, 3, (1, 2))
    send_squares(0)
    send_half(0, (1, 2))
    w_pass(2)
    ring_step(1, 3)
    finish_kv(0)
    ring_step(1, 4)
    ring_end(1)
    for ys in range(4):
        scale(1, ys)
        project(1, ys, (1, 2))
    send_squares(1)
    send_half(1, (1, 2))
    w_land(2)
    for b in range(2):
        for ys in range(4):
            project(b, ys, (0,))
        send_half(b, (0,))
    finish_kv(1)
    finish_q(0)
    finish_q(1)
    kv_wait(0)

    factor = 2.0 * HEAD ** -0.5

    def attend(b):
        @pl.loop(0, 3)
        def _(qc):
            rows = pl.ds(pl.multiple_of(qc * 128, 128), 128)
            query = qbuf[b, rows, :]

            def weights(ys, kb):
                score = lax.dot_general(
                    query, kvall[ys, kb, 0], (((1,), (1,)), ((), ())), preferred_element_type=F32
                )
                return jnp.exp(score * factor)

            def add(carry, weight, ys, kb):
                num, den = carry
                den = den + jnp.sum(weight, axis=1, keepdims=True)
                return num + dot(weight.astype(BF16), kvall[ys, kb, 1]), den

            def full(kb):
                return lambda ys, carry: add(carry, weights(ys, kb), ys, kb)

            carry = (jnp.zeros((128, HEAD), F32), jnp.zeros((128, 1), F32))
            if b == 1:
                carry = lax.fori_loop(0, 4, full(0), carry)
            carry = lax.fori_loop(0, y, full(b), carry)
            weight = weights(y, b)
            at = qc * 128 + lax.broadcasted_iota(jnp.int32, (128, T), 0)
            key = lax.broadcasted_iota(jnp.int32, (128, T), 1)
            weight = jnp.where(key <= at, weight, 0.0)
            num, den = add(carry, weight, y, b)
            oloc[b, rows, :] = (num / den).astype(BF16)

    attend(0)
    kv_wait(1)
    attend(1)

    here = pl.ds(pl.multiple_of(xh * HEAD, HEAD), HEAD)
    there = pl.ds(pl.multiple_of((1 - xh) * HEAD, HEAD), HEAD)
    o_copy = remote(oloc.at[1 - xh], obuf, o_s, o_r, x_far)
    o_copy.start()
    att_out[:, here] = oloc[xh]
    o_copy.wait_recv()
    att_out[:, there] = obuf[...]

    @pl.when(c < 7)
    def _():
        id_copy().wait_send()

    for e in range(2):
        me = (xl == xh) & (z // 2 == y) & (2 * y + e == z)

        @pl.when(jnp.logical_not(me))
        def _():
            sc_copy(e)[2].wait_send()

    for a in range(2):
        me = (xl == xh) & (xl == a)

        @pl.when(jnp.logical_not(me))
        def _():
            for h in range(2):
                e1_copy(a, h)[2].wait_send()

    for part in range(3):
        for d in (1, -1):
            w_copy(part, d).wait_send()
            w_forward(part, d).wait_send()
    for d in order:
        az_copy(d).wait_send()
    for d in range(8):
        ax_copy(d).wait_send()
        ac_copy(d, 0).wait_send()
        ac_copy(d, 1).wait_send()
    for d in range(1, 8):
        for kind in range(3):
            rs_copy(kind, d).wait_send()
        for kind in range(2):
            ag_copy(kind, d).wait_send()
    for b in range(2):
        for s in range(4):
            for h in range(2):
                if s < 3 or h == 0:
                    zr_copy(b, s, h).wait_send()
                if s < 3 or h == 1:
                    zl_copy(b, s, h).wait_send()
        for s in range(8):
            for h in range(2):
                sib_copy(b, s, h).wait_send()
        for m in range(4):
            g_copy(b, m).wait_send()
        for d in range(1, 4):
            kv_copy(b, d).wait_send()
    o_copy.wait_send()


def local(base_ids, embedding, first_gain, hyena_weight, short_filter, long_filter, second_gain, attn_weight):
    dma = pltpu.SemaphoreType.DMA
    vmem = pltpu.VMEM
    scratch = [
        vmem((T,), jnp.int32),
        vmem((2, V, 2 * C), BF16),
        vmem((V, KD), BF16),
        vmem((V, 2 * C), BF16),
        vmem((V, C), BF16),
        vmem((1, V), F32),
        vmem((7, 64, 2 * C), BF16),
        vmem((7, 64, C), BF16),
        vmem((7, 1, V), F32),
        vmem((V, 2 * C), BF16),
        vmem((V, C), BF16),
        vmem((640, 3 * C), F32),
        vmem((2, 512, 128), F32),
        vmem((T // 8 + LONG, 8, 128), F32),
        vmem((T, 128), F32),
        vmem((2, T, 128), BF16),
        vmem((4, 3, KD, C), BF16),
        vmem((2, T, 16 * C), BF16),
        vmem((2, T, 16 * C), BF16),
        vmem((2, T, 3 * C), F32),
        vmem((2, V, 128), F32),
        vmem((2, 3, T, HEAD), BF16),
        vmem((2, 3, T, HEAD), BF16),
        vmem((2, 1, T), F32),
        vmem((2, 1, T), F32),
        vmem((2, T, HEAD), BF16),
        vmem((4, 2, 2, T, HEAD), BF16),
        vmem((2, T, HEAD), BF16),
        vmem((T, HEAD), BF16),
        dma, dma,
        dma((2,)), dma((2,)),
        dma((8,)), dma((8,)),
        dma((8,)), dma((8,)),
        dma((2, 8)), dma((2, 8)),
        dma((3, 7)), dma((3, 7)),
        dma((2, 7)), dma((2, 7)),
        dma((3, 2, 2)), dma((3, 2, 2)), dma,
        dma((2, 2)), dma((2, 2)),
        dma((2, 4, 2)), dma((2, 4, 2)),
        dma((2, 4, 2)), dma((2, 4, 2)),
        dma((2, 8, 2)), dma((2, 8, 2)),
        dma((2, 4)), dma((2, 4)),
        dma((2, 3)), dma((2, 3)),
        dma, dma,
    ]
    return pl.pallas_call(
        kernel,
        out_shape=(jax.ShapeDtypeStruct((T, C), BF16), jax.ShapeDtypeStruct((T, C), BF16)),
        in_specs=[pl.BlockSpec(memory_space=pltpu.VMEM)] * 8,
        out_specs=(pl.BlockSpec(memory_space=pltpu.VMEM), pl.BlockSpec(memory_space=pltpu.VMEM)),
        scratch_shapes=scratch,
        compiler_params=pltpu.CompilerParams(
            collective_id=0, has_side_effects=True, vmem_limit_bytes=56 << 20
        ),
    )(
        base_ids,
        embedding,
        first_gain,
        jnp.transpose(hyena_weight, (1, 0, 2)),
        short_filter,
        long_filter,
        second_gain,
        jnp.transpose(attn_weight, (1, 0, 2)),
    )


def solution(mesh):
    return jax.shard_map(
        local,
        mesh=mesh,
        in_specs=(
            P("ctx"),
            P(None, "fsdp"),
            P(),
            P("ctx", None, "fsdp"),
            P(None, None, "fsdp"),
            P(None, "fsdp"),
            P(),
            P("ctx", None, "fsdp"),
        ),
        out_specs=(P("ctx", "fsdp"), P("ctx", "fsdp")),
        check_vma=False,
    )
```

time: 183 us -> 141 us (0.77)
  Pallas kernels: 172 us -> 136 us
  local copies, waits for them, and re-layouts: 8.59 us -> 3.23 us
    pallas_call x1, Pallas kernels: 172 us -> 136 us  [local(): pl.pallas_call(kernel, out_shape=(jax.ShapeDtypeStruct((T, C), BF16), jax...]
    reshape x4 -> x0, local copies, waits for them, and re-layouts: 5.35 us -> none  [the longest x1 1.38 us: local(): first_gain.reshape(8, KD)]
where the time goes in v2:
time: 141 us; the launch traced here: 140 us
  Pallas kernels  136 us (96%)
  local copies, waits for them, and re-layouts  3.23 us (2%)
    pallas_call x1, Pallas kernels, local(): pl.pallas_call(kernel, out_shape=(jax.ShapeDtypeStruct((T, C), BF16), jax...  136 us
    unnamed x2, local copies, waits for them, and re-layouts  3.23 us

profile of v2, /device:TPU:28, one launch (start us, length us, event | category | flops | bytes accessed | tf_op | source)
XLA Modules:
  0.0 139.8 jit_solution(17065769319528815018)
XLA Ops:
  0.6 136.0 %shard_map.95 = (bf16[384,256]{1,0:T(8,128)(2,1)}, bf16[384,256]{1,0:T(8,128)(2,1)}) custom-call(s32[384]{0:T(512)} %ids.1, bf16[512,256]{1,0:T(8,128)(2,1)} %emb.1, f32[8192]{0:T(1024)} %g1.1, bf16[3,1024,256]{2,1,0:T(8,128)(2,1)} %bitcast.2, f32[3,3,256]{2,1,0:T(4,128)} %sf.1, f32[128,256]{1,0:T(8,128)} %lf.1, f32[8192]{0:T(1024)} %g2.1, ...), custom_call_target="tpu_custom_call" | custom-call | tf_op jit(solution)/shard_map/pallas_call | solution.py:612
  136.6 1.6 %copy.12 = bf16[384,256]{1,0:T(8,128)(2,1)} copy(bf16[384,256]{1,0:T(8,128)(2,1)} %get-tuple-element.4) | data formatting | bytes 393216
  138.2 1.6 %copy.13 = bf16[384,256]{1,0:T(8,128)(2,1)} copy(bf16[384,256]{1,0:T(8,128)(2,1)} %get-tuple-element.5) | data formatting | bytes 393216

commit v3 on v2

v3 whole, which is shorter than its diff:
```python
import math

import jax
import jax.numpy as jnp
from jax import lax
from jax.experimental import pallas as pl
from jax.experimental.pallas import tpu as pltpu
from jax.sharding import PartitionSpec as P

MESH = pl.DeviceIdType.MESH
F32, BF16 = jnp.float32, jnp.bfloat16
T = 384
V = 512
C = 256
KD = 1024
D = 8192
HEAD = 128
LONG = 128
EPS = 1e-6


def dot(a, b):
    return jnp.dot(a, b, preferred_element_type=F32)


def kernel(
    ids, emb, g1, w1, sf, lf, g2, w2,
    mixed_out, att_out,
    idbuf, ebuf, xbuf, pkv, pq, psq, rskv, rsq, rssq, tkv, tq, sbuf, prbuf, taps, coef, xo, xu, xsum, dv, lcbuf, mbuf,
    w2all, mall, xs, pp, ssb, gs, gr, sqs, sqr, qbuf, kvall, num, den, oloc, obuf,
    id_s, id_r, sc_s, sc_r, az_s, az_r, ax_s, ax_r, ac_s, ac_r,
    rs_s, rs_r, ag_s, ag_r, w_s, w_r, wl_s, e1_s, e1_r, zr_s, zr_r, zl_s, zl_r, sw_s, sw_r, sib_s, sib_r,
    g_s, g_r, kv_s, kv_r, o_s, o_r,
):
    c = lax.axis_index("ctx")
    f = lax.axis_index("fsdp")
    xh, y = c // 4, c % 4
    xl, z, k = f // 16, (f // 2) % 8, f % 2

    def dev(xh_, y_, xl_, z_, k_):
        return (xh_ * 4 + y_, xl_ * 16 + z_ * 2 + k_)

    def ctx_peer(d):
        return ((c + d) % 8, f)

    def z_peer(d):
        return dev(xh, y, xl, (z + d) % 8, k)

    def y_peer(d):
        return dev(xh, (y + d) % 4, xl, z, k)

    x_sib = dev(xh, y, 1 - xl, z, k)
    core_sib = dev(xh, y, xl, z, 1 - k)
    x_far = dev(1 - xh, y, xl, z, k)

    def remote(src, dst, ss, rs, to):
        return pltpu.make_async_remote_copy(
            src_ref=src, dst_ref=dst, send_sem=ss, recv_sem=rs, device_id=to, device_id_type=MESH
        )

    barrier = pltpu.get_barrier_semaphore()
    count = 0
    peers = [ctx_peer(d) for d in range(1, 8)] + [z_peer(d) for d in range(1, 8)] + [x_sib, core_sib]
    peers += [dev(xl, z // 2, xh, 2 * ((y + 4 - z // 2) % 4) + e, k) for e in range(2)]
    peers += [dev(xl, (y + z // 2) % 4, xh, 2 * y + e, k) for e in range(2)]
    peers += [dev(xl, y, a, z, k) for a in range(2)]
    peers += [dev(a, y, xh, z, k) for a in range(2)]
    for p in peers:
        pl.semaphore_signal(barrier, inc=1, device_id=p, device_id_type=MESH)
        count += 1
    pl.semaphore_wait(barrier, count)

    def id_copy():
        return remote(ids, idbuf, id_s, id_r, ctx_peer(1))

    @pl.when(c < 7)
    def _():
        id_copy().start()

    rows_of = lambda xl_, z_: pl.ds(pl.multiple_of(xl_ * 256 + z_ * 32, 32), 32)

    def sc_copy(e):
        to_z = 2 * ((y + 4 - z // 2) % 4) + e
        rows = rows_of(xh, to_z)
        cols = pl.ds(pl.multiple_of((z % 2) * C, C), C)
        src, dst = emb.at[rows, :], ebuf.at[k, rows, cols]
        same = (xl == xh) & (z // 2 == y) & (to_z == z)
        return same, src, dst, remote(src, dst, sc_s.at[e], sc_r.at[z % 2], dev(xl, z // 2, xh, to_z, k))

    for e in range(2):
        same, src, dst, cp = sc_copy(e)

        @pl.when(same)
        def _():
            pltpu.make_async_copy(src, dst, sc_r.at[z % 2]).start()

        @pl.when(jnp.logical_not(same))
        def _():
            cp.start()

    W_PARTS = ((1, 3, 0, 640), (1, 3, 640, KD - 640), (0, 1, 0, KD))

    def w_copy(part, d):
        m0, m1, row, count_ = W_PARTS[part]
        side = {1: 0, -1: 1}[d]
        cut = (slice(m0, m1), slice(row, row + count_), slice(None))
        return remote(
            w2.at[cut], w2all.at[cut[0], y, cut[1]], w_s.at[part, 0, side], w_r.at[part, 0, side], y_peer(d)
        )

    def w_forward(part, d):
        m0, m1, row, count_ = W_PARTS[part]
        side = {1: 0, -1: 1}[d]
        half = count_ // 2
        piece = w2all.at[m0:m1, (y - d) % 4, row + side * half : row + (side + 1) * half, :]
        return remote(piece, piece, w_s.at[part, 1, side], w_r.at[part, 1, side], y_peer(d))

    def w_send(part):
        for d in (1, -1):
            w_copy(part, d).start()

    def w_pass(part):
        for d in (1, -1):
            w_copy(part, d).wait_recv()
            w_forward(part, d).start()

    def w_land(part):
        for d in (1, -1):
            w_forward(part, d).wait_recv()

    w_local = pltpu.make_async_copy(w2, w2all.at[:, y], wl_s)
    w_local.start()
    w_send(0)

    def taps_of(lt):
        taps[...] = lf[:, lt * 128 : (lt + 1) * 128]
        even, odd = taps[pl.ds(0, LONG // 2, stride=2), :], taps[pl.ds(1, LONG // 2, stride=2), :]
        coef[lt, 0] = even
        coef[lt, 1] = odd
        coef[lt, 2] = even + odd

    taps_of(0)
    taps_of(1)

    for zb in range(2):
        rows = rows_of(xl, z)
        piece = ebuf.at[k, rows, pl.ds(zb * C, C)]
        remote(piece, piece, sc_s.at[zb], sc_r.at[zb], core_sib).wait_recv()

    def az_copy(d):
        piece = ebuf.at[k, rows_of(xl, z), :]
        return remote(piece, piece, az_s.at[d], az_r.at[d], z_peer(d))

    def ax_copy(d):
        piece = ebuf.at[k, rows_of(xl, (z - d) % 8), :]
        return remote(piece, piece, ax_s.at[d], ax_r.at[d], x_sib)

    def ac_copy(d, s):
        xl_ = (xl + s) % 2
        piece = ebuf.at[k, rows_of(xl_, (z - d) % 8), :]
        return remote(piece, piece, ac_s.at[s, d], ac_r.at[s, d], core_sib)

    order = (1, 7, 2, 6, 3, 5, 4)
    for d in order:
        az_copy(d).start()
    ax_copy(0).start()
    ac_copy(0, 0).start()
    for d in order:
        az_copy(d).wait_recv()
        ax_copy(d).start()
        ac_copy(d, 0).start()
    gain = g1[pl.ds(pl.multiple_of(c * KD, KD), KD)].reshape(1, KD)
    mine = pl.ds(pl.multiple_of(c * 64, 64), 64)

    def half_rows(hv):
        return pl.ds(pl.multiple_of(((xl + hv) % 2) * 256, 256), 256)

    def table(hv):
        rows = half_rows(hv)
        squares = jnp.zeros((256, 1), F32)
        for q in range(4):
            e = ebuf[q % 2, rows, (q // 2) * C : (q // 2 + 1) * C].astype(F32)
            squares = squares + jnp.sum(e * e, axis=1, keepdims=True)
            xbuf[:, q * C : (q + 1) * C] = (e * gain[:, q * C : (q + 1) * C]).astype(BF16)
        psq[hv] = jnp.transpose(jnp.broadcast_to(squares, (256, 128)))[0:1, :]
        terms = [dot(xbuf[...], w1[m]).astype(BF16) for m in (1, 2, 0)]
        pkv[rows, :C] = terms[0]
        pkv[rows, C:] = terms[1]
        pq[rows, :] = terms[2]

    def rs_copy(kind, hv, dy):
        half = (xl + hv) % 2
        to = half * 4 + (y + dy) % 4
        rows = pl.ds(pl.multiple_of(to * 64, 64), 64)
        src = (pkv.at[rows, :], pq.at[rows, :], psq.at[hv])[kind]
        dst = (rskv, rsq, rssq)[kind].at[c]
        return remote(src, dst, rs_s.at[kind, hv, dy], rs_r.at[kind, c], (to, f))

    def rs_each(hv, kinds, act):
        for kind in kinds:
            for dy in (2, 1, 3):
                act(rs_copy(kind, hv, dy))

            @pl.when((xl + hv) % 2 != xh)
            def _():
                act(rs_copy(kind, hv, 0))

    def rs_land(kind):
        slots = []
        for dx in (0, 1):
            for dy in (0, 1, 2, 3):
                if (dx, dy) != (0, 0):
                    slot = ((xh + dx) % 2) * 4 + (y + dy) % 4
                    src = (pkv.at[mine, :], pq.at[mine, :], psq.at[0])[kind]
                    dst = (rskv, rsq, rssq)[kind].at[slot]
                    remote(src, dst, rs_s.at[kind, 0, 0], rs_r.at[kind, slot], core_sib).wait_recv()
                    slots.append(slot)
        return slots

    def ag_copy(kind, d):
        piece = (tkv, tq)[kind].at[mine, :]
        return remote(piece, piece, ag_s.at[kind, d - 1], ag_r.at[kind, d - 1], ctx_peer(d))

    ctx_order = (4, 1, 7, 2, 6, 3, 5)
    for d in (0,) + order:
        ac_copy(d, 0).wait_recv()
    table(0)
    rs_each(0, (2, 0, 1), lambda copy: copy.start())
    for d in (0,) + order:
        ax_copy(d).wait_recv()
        ac_copy(d, 1).start()
    for d in (0,) + order:
        ac_copy(d, 1).wait_recv()
    table(1)
    rs_each(1, (2, 0, 1), lambda copy: copy.start())
    sq = psq[(xl + xh) % 2]
    for slot in rs_land(2):
        sq = sq + rssq[slot]
    row = lax.rsqrt(sq / D + EPS)
    ssb[0, :256, :] = jnp.transpose(jnp.broadcast_to(row, (128, 256)))
    scale_row = ssb[0, pl.ds(pl.multiple_of(y * 64, 64), 64), :][:, 0:1]
    total = pkv[mine, :].astype(F32)
    for slot in rs_land(0):
        total = total + rskv[slot].astype(F32)
    tkv[mine, :] = (total * scale_row).astype(BF16)
    for d in ctx_order:
        ag_copy(0, d).start()
    total = pq[mine, :].astype(F32)
    for slot in rs_land(1):
        total = total + rsq[slot].astype(F32)
    tq[mine, :] = (total * scale_row).astype(BF16)
    for d in ctx_order:
        ag_copy(1, d).start()

    @pl.when(c > 0)
    def _():
        id_copy().wait_recv()

    @pl.when(c == 0)
    def _():
        idbuf[...] = jnp.full(idbuf.shape, -1, jnp.int32)

    for d in ctx_order:
        ag_copy(0, d).wait_recv()

    w_pass(0)
    w_send(1)
    def one_hot(chunk):
        row = idbuf[128 + chunk * 128 : 256 + chunk * 128] if chunk < 2 else ids[(chunk - 2) * 128 : (chunk - 1) * 128]
        words = lax.broadcasted_iota(jnp.int32, (V, 128), 0)
        return jnp.where(words == row.reshape(1, 128), 1.0, 0.0).astype(BF16)

    def pick(hot, values):
        return lax.dot_general(hot, values, (((0,), (0,)), ((), ())), preferred_element_type=F32)

    for chunk in range(5):
        sbuf[chunk * 128 : (chunk + 1) * 128, C:] = pick(one_hot(chunk), tkv[...])

    def short(m, start, size, lanes=slice(0, C)):
        cols = slice(m * C + lanes.start, m * C + lanes.stop)
        out = sf[0, m : m + 1, lanes] * sbuf[start : start + size, cols]
        for j in range(1, 3):
            out = out + sf[j, m : m + 1, lanes] * sbuf[start - j : start - j + size, cols]
        return out

    for chunk in range(4):
        prod = (short(1, 128 + chunk * 128, 128) * short(2, 128 + chunk * 128, 128)).astype(BF16).astype(F32)
        for lt in range(2):
            prbuf[lt, chunk * 128 : (chunk + 1) * 128, :] = prod[:, lt * 128 : (lt + 1) * 128]

    def cols_of(z_, k_, h):
        return pl.ds(pl.multiple_of((z_ * 2 + k_) * C + h * 128, 128), 128)

    def rows_at(h, half):
        return pl.ds(0, T) if h == 0 else pl.ds(pl.multiple_of(half * (T // 2), T // 2), T // 2)

    def e1_copy(a, h):
        dst = mall.at[xh, rows_at(h, a), cols_of(z, k, h)]
        src = mbuf.at[h, rows_at(h, a), :]
        return src, dst, remote(src, dst, e1_s.at[a, h], e1_r.at[xh, h], dev(xl, y, a, z, k))

    def e1_send(h):
        for a in range(2):
            src, dst, cp = e1_copy(a, h)
            me = (xl == xh) & (xl == a)

            @pl.when(me)
            def _():
                pltpu.make_async_copy(src, dst, e1_r.at[xh, h]).start()

            @pl.when(jnp.logical_not(me))
            def _():
                cp.start()

    LANE_T = T // 8

    def half_filter(lt, which, src, start, count_):
        def eight(k8, acc):
            window = src[pl.ds(start + 56 - 8 * k8, count_ + 7)]
            row = coef[lt, which, pl.ds(pl.multiple_of(8 * k8, 8), 8), :]
            for jj in range(8):
                acc = acc + row[jj : jj + 1, :][None] * window[7 - jj : count_ + 7 - jj]
            return acc

        return lax.fori_loop(0, LONG // 16, eight, jnp.zeros((count_, 8, 128), F32), unroll=True)

    def convolve(lt):
        xu[0] = prbuf[lt, pl.ds(1, 8, stride=LANE_T), :]
        for m in range(87):
            odd = prbuf[lt, pl.ds(2 * m + 2, 8, stride=LANE_T), :]
            even = prbuf[lt, pl.ds(2 * m + 3, 8, stride=LANE_T), :]
            xo[m] = odd
            xu[m + 1] = even
            xsum[m] = odd + even
        dv[0:13] = half_filter(lt, 1, xu, 0, 13)
        dv[13:25] = half_filter(lt, 1, xu, 13, 12)
        for g in range(2):
            a = half_filter(lt, 0, xo, 12 * g, 12)
            t = half_filter(lt, 2, xsum, 12 * g, 12)
            for i in range(12):
                n = 12 * g + i
                lcbuf[pl.ds(2 * n, 8, stride=LANE_T), :] = a[i] + dv[n]
                lcbuf[pl.ds(2 * n + 1, 8, stride=LANE_T), :] = t[i] - a[i] - dv[n + 1]

    def residual(lt):
        lanes = slice(lt * 128, (lt + 1) * 128)
        for chunk in range(3):
            rows = slice(chunk * 128, (chunk + 1) * 128)
            features = pick(one_hot(chunk + 2), emb[:, lanes])
            gate = short(0, 256 + chunk * 128, 128, lanes)
            mixed = (features + gate * lcbuf[rows, :]).astype(BF16)
            mbuf[lt, rows, :] = mixed
            mixed_out[rows, lanes] = mixed

    convolve(0)
    for d in ctx_order:
        ag_copy(1, d).wait_recv()
    for chunk in range(1, 5):
        sbuf[chunk * 128 : (chunk + 1) * 128, :C] = pick(one_hot(chunk), tq[...])
    residual(0)
    e1_send(0)
    convolve(1)
    residual(1)
    e1_send(1)

    def chunk_of(b, z_, p):
        rows = rows_at(1, xl) if p == 2 else pl.ds(p * (T // 2), T // 2)
        return mall.at[b, rows, cols_of(z_, k, p // 2)]

    def zr_copy(b, s, p):
        piece = chunk_of(b, (z + 8 - s) % 8, p)
        return remote(piece, piece, zr_s.at[b, s, p], zr_r.at[b, s, p], z_peer(1))

    def zl_copy(b, s, p):
        piece = chunk_of(b, (z + s) % 8, p)
        return remote(piece, piece, zl_s.at[b, s, p], zl_r.at[b, s, p], z_peer(-1))

    def sib_copy(b, s, h):
        piece = mall.at[b, rows_at(h, xl), cols_of((z + s) % 8, k, h)]
        return remote(piece, piece, sib_s.at[b, s, h], sib_r.at[b, s, h], core_sib)

    def swap_copy(b, s):
        piece = mall.at[b, rows_at(1, xl), cols_of((z + s) % 8, k, 1)]
        return remote(piece, piece, sw_s.at[b, s], sw_r.at[b, s], x_sib)

    def sib2_copy(b, s):
        piece = mall.at[b, rows_at(1, 1 - xl), cols_of((z + s) % 8, k, 1)]
        return remote(piece, piece, sib_s.at[b, s, 2], sib_r.at[b, s, 2], core_sib)

    def share(b, s, p):
        if p > 0:
            sib_copy(b, s, p - 1).start()
        if p == 2:
            swap_copy(b, s).start()

    def swap_land(b, s):
        swap_copy(b, s).wait_recv()
        sib2_copy(b, s).start()

    def ring_start(b, h):
        piece = mall.at[b, rows_at(h, xl), cols_of(z, k, h)]
        remote(piece, piece, e1_s.at[0, h], e1_r.at[b, h], core_sib).wait_recv()
        for p in ((0, 1), (2,))[h]:
            zr_copy(b, 0, p).start()
            zl_copy(b, 0, p).start()
        share(b, 0, h + 1)

    def goes_right(s, p):
        return s < 3 or (s == 3 and p < 2)

    def goes_left(s, p):
        return s < 3 or (s == 3 and p == 2)

    def ring_step(b, s):
        for p in range(3):
            if goes_right(s - 1, p):
                zr_copy(b, s - 1, p).wait_recv()
                if goes_right(s, p):
                    zr_copy(b, s, p).start()
            if goes_left(s - 1, p):
                zl_copy(b, s - 1, p).wait_recv()
                if goes_left(s, p):
                    zl_copy(b, s, p).start()
            if goes_right(s - 1, p):
                share(b, 8 - s, p)
            if goes_left(s - 1, p) and s < 4 or s == 4 and p == 2:
                share(b, s, p)
        if s == 2:
            swap_land(b, 0)
        if s > 2:
            swap_land(b, 8 - (s - 2))
            swap_land(b, s - 2)

    def ring_end(b):
        for s in (5, 3, 4):
            swap_land(b, s)
        for s in range(8):
            for h in range(2):
                sib_copy(b, s, h).wait_recv()
            sib2_copy(b, s).wait_recv()

    def scale(b, ys):
        gain2 = g2[pl.ds(pl.multiple_of((4 * xh + ys) * KD, KD), KD)].reshape(1, KD)
        cols = pl.ds(pl.multiple_of(ys * KD, KD), KD)
        for r in range(3):
            rows = slice(r * 128, (r + 1) * 128)
            part = mall[b, rows, cols].astype(F32)
            squares_ = jnp.broadcast_to(jnp.sum(part * part, axis=1, keepdims=True), (128, 128))
            ssb[b, rows, :] = squares_ if ys == 0 else ssb[b, rows, :] + squares_
            xs[b, rows, cols] = (part * gain2).astype(BF16)

    def project(pairs):
        terms = [dot(xs[b], w2all[m].reshape(4 * KD, C)) for b, m in pairs]
        for (b, m), term in zip(pairs, terms):
            pp[b, :, m * C : (m + 1) * C] = term

    def g_copy(b, m):
        if m == 3:
            return remote(sqs.at[b], sqr.at[b], g_s.at[b, m], g_r.at[b, m], x_far)
        return remote(gs.at[b, m], gr.at[b, m], g_s.at[b, m], g_r.at[b, m], x_far)

    def head_cols(m, h):
        return pl.ds(pl.multiple_of(m * C + h * HEAD, HEAD), HEAD)

    def send_half(b, ms):
        for m in ms:
            gs[b, m] = pp[b, :, head_cols(m, 1 - xh)].astype(BF16)
            g_copy(b, m).start()

    def send_squares(b):
        sqs[b] = jnp.transpose(ssb[b, :T, :])[0:1, :]
        g_copy(b, 3).start()

    def row_factor(b):
        g_copy(b, 3).wait_recv()
        other = jnp.transpose(jnp.broadcast_to(sqr[b], (128, T)))
        ssb[b, :T, :] = lax.rsqrt((ssb[b, :T, :] + other) / D + EPS)

    def head_norm(values):
        values = values.astype(F32)
        return (values * lax.rsqrt(jnp.mean(values * values, axis=1, keepdims=True) + EPS)).astype(BF16)

    def kv_copy(b, d):
        block = kvall.at[y, b]
        side = {1: 0, -1: 1}[d]
        return remote(block, block, kv_s.at[b, side], kv_r.at[b, side], y_peer(d))

    def kv_forward(b, d):
        side = {1: 0, -1: 1}[d]
        part = kvall.at[(y + 4 - d) % 4, b, side]
        return remote(part, part, kv_s.at[b, 2 + side], kv_r.at[b, 2 + side], y_peer(d))

    def kv_pass(b):
        for d in (1, -1):
            kv_copy(b, d).wait_recv()
            kv_forward(b, d).start()

    def kv_land(b):
        for d in (1, -1):
            kv_forward(b, d).wait_recv()

    def joined(b, m):
        g_copy(b, m).wait_recv()
        return ((pp[b, :, head_cols(m, xh)] + gr[b, m].astype(F32)) * ssb[b, :T, :]).astype(BF16)

    def finish_kv(b):
        row_factor(b)
        kvall[y, b, 0] = head_norm(joined(b, 1))
        kvall[y, b, 1] = joined(b, 2)
        for d in (1, -1):
            kv_copy(b, d).start()

    def finish_q(b):
        qbuf[b] = head_norm(joined(b, 0))

    for h in range(2):
        for b in range(2):
            ring_start(b, h)
    ring_step(0, 1)
    ring_step(1, 1)
    ring_step(0, 2)
    w_pass(1)
    w_send(2)
    ring_step(1, 2)
    ring_step(0, 3)
    ring_step(1, 3)
    ring_step(0, 4)
    ring_step(1, 4)
    ring_end(0)
    for ys in range(4):
        scale(0, ys)
    send_squares(0)
    w_local.wait()
    w_land(0)
    w_land(1)
    project(((0, 1), (0, 2)))
    send_half(0, (1, 2))
    w_pass(2)
    ring_end(1)
    for ys in range(4):
        scale(1, ys)
    send_squares(1)
    project(((1, 1), (1, 2)))
    send_half(1, (1, 2))
    finish_kv(0)
    w_land(2)
    project(((0, 0), (1, 0)))
    send_half(0, (0,))
    send_half(1, (0,))
    kv_pass(0)
    finish_kv(1)
    finish_q(0)
    finish_q(1)
    kv_land(0)

    factor = 2.0 * HEAD ** -0.5 * math.log2(math.e)

    def key_block(b, ys, kb, diagonal=False, first=False):
        for qc in range(3):
            rows = slice(qc * 128, (qc + 1) * 128)
            width = (qc + 1) * 128 if diagonal else T
            score = lax.dot_general(
                qbuf[b, rows, :], kvall[ys, kb, 0, :width, :], (((1,), (1,)), ((), ())), preferred_element_type=F32
            )
            weight = jnp.exp2(score * factor)
            if diagonal:
                at = qc * 128 + lax.broadcasted_iota(jnp.int32, (128, width), 0)
                key = lax.broadcasted_iota(jnp.int32, (128, width), 1)
                weight = jnp.where(key <= at, weight, 0.0)
            part = weight[:, :128]
            for n in range(1, width // 128):
                part = part + weight[:, n * 128 : (n + 1) * 128]
            term = dot(weight.astype(BF16), kvall[ys, kb, 1, :width, :])
            if first:
                den[b, rows, :] = part
                num[b, rows, :] = term
            else:
                den[b, rows, :] += part
                num[b, rows, :] += term

    def earlier(b):
        @pl.loop(0, y)
        def _(ys):
            key_block(b, ys, b)

    def o_copy(b, chunk):
        rows = slice(chunk * 128, (chunk + 1) * 128)
        return remote(oloc.at[b, rows, :], obuf.at[rows, :], o_s.at[chunk], o_r.at[chunk], x_far)

    here = pl.ds(pl.multiple_of(xh * HEAD, HEAD), HEAD)
    there = pl.ds(pl.multiple_of((1 - xh) * HEAD, HEAD), HEAD)

    def conclude(b):
        for chunk in range(3):
            rows = slice(chunk * 128, (chunk + 1) * 128)
            out = num[b, rows, :] / jnp.sum(den[b, rows, :], axis=1, keepdims=True)
            oloc[b, rows, :] = out.astype(BF16)

            @pl.when(xh == 1 - b)
            def _():
                o_copy(b, chunk).start()

            @pl.when(xh == b)
            def _():
                att_out[rows, here] = oloc[b, rows, :]

    key_block(0, y, 0, diagonal=True, first=True)
    earlier(0)
    conclude(0)
    kv_pass(1)
    key_block(1, 0, 0, first=True)

    @pl.loop(1, 4)
    def _(ys):
        key_block(1, ys, 0)

    kv_land(1)
    key_block(1, y, 1, diagonal=True)
    earlier(1)
    conclude(1)
    for chunk in range(3):
        o_copy(0, chunk).wait_recv()
    att_out[:, there] = obuf[...]

    @pl.when(c < 7)
    def _():
        id_copy().wait_send()

    for e in range(2):
        same, _, _, cp = sc_copy(e)

        @pl.when(jnp.logical_not(same))
        def _():
            cp.wait_send()

    for a in range(2):
        me = (xl == xh) & (xl == a)

        @pl.when(jnp.logical_not(me))
        def _():
            for h in range(2):
                e1_copy(a, h)[2].wait_send()

    for part in range(3):
        for d in (1, -1):
            w_copy(part, d).wait_send()
            w_forward(part, d).wait_send()
    for d in order:
        az_copy(d).wait_send()
    for d in range(8):
        ax_copy(d).wait_send()
        ac_copy(d, 0).wait_send()
        ac_copy(d, 1).wait_send()
    for d in range(1, 8):
        for kind in range(2):
            ag_copy(kind, d).wait_send()
    for hv in range(2):
        rs_each(hv, range(3), lambda copy: copy.wait_send())
    for b in range(2):
        for s in range(4):
            for p in range(3):
                if goes_right(s, p):
                    zr_copy(b, s, p).wait_send()
                if goes_left(s, p):
                    zl_copy(b, s, p).wait_send()
        for s in range(8):
            for h in range(2):
                sib_copy(b, s, h).wait_send()
            sib2_copy(b, s).wait_send()
            swap_copy(b, s).wait_send()
        for m in range(4):
            g_copy(b, m).wait_send()
        for d in (1, -1):
            kv_copy(b, d).wait_send()
            kv_forward(b, d).wait_send()
    for chunk in range(3):
        o_copy(0, chunk).wait_send()


def hand_over(mixed, att, mixed_out, att_out):
    mixed_out[...] = mixed[...]
    att_out[...] = att[...]


def local(base_ids, embedding, first_gain, hyena_weight, short_filter, long_filter, second_gain, attn_weight):
    dma = pltpu.SemaphoreType.DMA
    vmem = pltpu.VMEM
    scratch = [
        vmem((T,), jnp.int32),
        vmem((2, V, 2 * C), BF16),
        vmem((256, KD), BF16),
        vmem((V, 2 * C), BF16),
        vmem((V, C), BF16),
        vmem((2, 1, 256), F32),
        vmem((8, 64, 2 * C), BF16),
        vmem((8, 64, C), BF16),
        vmem((8, 1, 256), F32),
        vmem((V, 2 * C), BF16),
        vmem((V, C), BF16),
        vmem((640, 3 * C), F32),
        vmem((2, 512, 128), F32),
        vmem((LONG, 128), F32),
        vmem((2, 3, LONG // 2, 128), F32),
        vmem((88, 8, 128), F32),
        vmem((88, 8, 128), F32),
        vmem((88, 8, 128), F32),
        vmem((25, 8, 128), F32),
        vmem((T, 128), F32),
        vmem((2, T, 128), BF16),
        vmem((3, 4, KD, C), BF16),
        vmem((2, T, 16 * C), BF16),
        vmem((2, T, 16 * C), BF16),
        vmem((2, T, 3 * C), F32),
        vmem((2, V, 128), F32),
        vmem((2, 3, T, HEAD), BF16),
        vmem((2, 3, T, HEAD), BF16),
        vmem((2, 1, T), F32),
        vmem((2, 1, T), F32),
        vmem((2, T, HEAD), BF16),
        vmem((4, 2, 2, T, HEAD), BF16),
        vmem((2, T, HEAD), F32),
        vmem((2, T, HEAD), F32),
        vmem((2, T, HEAD), BF16),
        vmem((T, HEAD), BF16),
        dma, dma,
        dma((2,)), dma((2,)),
        dma((8,)), dma((8,)),
        dma((8,)), dma((8,)),
        dma((2, 8)), dma((2, 8)),
        dma((3, 2, 4)), dma((3, 8)),
        dma((2, 7)), dma((2, 7)),
        dma((3, 2, 2)), dma((3, 2, 2)), dma,
        dma((2, 2)), dma((2, 2)),
        dma((2, 4, 3)), dma((2, 4, 3)),
        dma((2, 4, 3)), dma((2, 4, 3)),
        dma((2, 8)), dma((2, 8)),
        dma((2, 8, 3)), dma((2, 8, 3)),
        dma((2, 4)), dma((2, 4)),
        dma((2, 4)), dma((2, 4)),
        dma((3,)), dma((3,)),
    ]
    results = pl.pallas_call(
        kernel,
        out_shape=(jax.ShapeDtypeStruct((T, C), BF16), jax.ShapeDtypeStruct((T, C), BF16)),
        in_specs=[pl.BlockSpec(memory_space=pltpu.VMEM)] * 8,
        out_specs=(pl.BlockSpec(memory_space=pltpu.VMEM), pl.BlockSpec(memory_space=pltpu.VMEM)),
        scratch_shapes=scratch,
        compiler_params=pltpu.CompilerParams(
            collective_id=0, has_side_effects=True, vmem_limit_bytes=56 << 20
        ),
    )(
        base_ids,
        embedding,
        first_gain,
        jnp.transpose(hyena_weight, (1, 0, 2)),
        short_filter,
        long_filter,
        second_gain,
        jnp.transpose(attn_weight, (1, 0, 2)),
    )
    shape = jax.ShapeDtypeStruct((T, C), BF16)
    return pl.pallas_call(hand_over, out_shape=(shape, shape))(*results)


def solution(mesh):
    return jax.shard_map(
        local,
        mesh=mesh,
        in_specs=(
            P("ctx"),
            P(None, "fsdp"),
            P(),
            P("ctx", None, "fsdp"),
            P(None, None, "fsdp"),
            P(None, "fsdp"),
            P(),
            P("ctx", None, "fsdp"),
        ),
        out_specs=(P("ctx", "fsdp"), P("ctx", "fsdp")),
        check_vma=False,
    )
```

time: 141 us -> 126 us (0.89)
  Pallas kernels: 136 us -> 125 us
  local copies, waits for them, and re-layouts: 3.23 us -> 0 us
    pallas_call x1, Pallas kernels: 136 us -> 123 us  [local(): pl.pallas_call(kernel, out_shape=(jax.ShapeDtypeStruct((T, C), BF16), jax...]
    unnamed x2 -> x0, local copies, waits for them, and re-layouts: 3.23 us -> none
    pallas_call x0 -> x1, Pallas kernels: none -> 1.78 us  [local(): return pl.pallas_call(hand_over, out_shape=(shape, shape))(*results)]
where the time goes in v3:
time: 126 us; the launch traced here: 125 us
  Pallas kernels  125 us (99%)
    pallas_call x1, Pallas kernels, local(): pl.pallas_call(kernel, out_shape=(jax.ShapeDtypeStruct((T, C), BF16), jax...  123 us

profile of v3, /device:TPU:28, one launch (start us, length us, event | category | flops | bytes accessed | tf_op | source)
XLA Modules:
  0.0 125.3 jit_solution(18256681687319400538)
XLA Ops:
  0.6 122.9 %shard_map.95 = (bf16[384,256]{1,0:T(8,128)(2,1)}, bf16[384,256]{1,0:T(8,128)(2,1)}) custom-call(s32[384]{0:T(512)} %ids.1, bf16[512,256]{1,0:T(8,128)(2,1)} %emb.1, f32[8192]{0:T(1024)} %g1.1, bf16[3,1024,256]{2,1,0:T(8,128)(2,1)} %bitcast.2, f32[3,3,256]{2,1,0:T(4,128)} %sf.1, f32[128,256]{1,0:T(8,128)} %lf.1, f32[8192]{0:T(1024)} %g2.1, ...), custom_call_target="tpu_custom_call" | custom-call | tf_op jit(solution)/shard_map/pallas_call | solution.py:742
  123.5 1.8 %shard_map.96 = (bf16[384,256]{1,0:T(8,128)(2,1)}, bf16[384,256]{1,0:T(8,128)(2,1)}) custom-call(bf16[384,256]{1,0:T(8,128)(2,1)} %get-tuple-element.4.mixed, bf16[384,256]{1,0:T(8,128)(2,1)} %get-tuple-element.5.att), custom_call_target="tpu_custom_call" | custom-call | tf_op jit(solution)/shard_map/pallas_call | solution.py:762

commit v4 on v3

--- a/solution.py
+++ b/solution.py
@@ -60,9 +60,9 @@
 
     barrier = pltpu.get_barrier_semaphore()
     count = 0
-    peers = [ctx_peer(d) for d in range(1, 8)] + [z_peer(d) for d in range(1, 8)] + [x_sib, core_sib]
-    peers += [dev(xl, z // 2, xh, 2 * ((y + 4 - z // 2) % 4) + e, k) for e in range(2)]
-    peers += [dev(xl, (y + z // 2) % 4, xh, 2 * y + e, k) for e in range(2)]
+    peers = [ctx_peer(d) for d in range(1, 8)] + [z_peer(d) for d in (1, 7, 2, 6)] + [x_sib, core_sib]
+    peers += [dev(xl, z // 2, xh, 2 * ((2 * (z // 2) + 6 - y) % 4) + e, k) for e in range(2)]
+    peers += [dev(xl, (2 * y + 6 - z // 2) % 4, xh, 2 * y + e, k) for e in range(2)]
     peers += [dev(xl, y, a, z, k) for a in range(2)]
     peers += [dev(a, y, xh, z, k) for a in range(2)]
     for p in peers:
@@ -77,10 +77,10 @@
     def _():
         id_copy().start()
 
-    rows_of = lambda xl_, z_: pl.ds(pl.multiple_of(xl_ * 256 + z_ * 32, 32), 32)
+    rows_of = lambda xl_, z_: pl.ds(pl.multiple_of(xl_ * 256 + (z_ % 4) * 64, 64), 64)
 
     def sc_copy(e):
-        to_z = 2 * ((y + 4 - z // 2) % 4) + e
+        to_z = 2 * ((2 * (z // 2) + 6 - y) % 4) + e
         rows = rows_of(xh, to_z)
         cols = pl.ds(pl.multiple_of((z % 2) * C, C), C)
         src, dst = emb.at[rows, :], ebuf.at[k, rows, cols]
@@ -98,7 +98,7 @@
         def _():
             cp.start()
 
-    W_PARTS = ((1, 3, 0, 640), (1, 3, 640, KD - 640), (0, 1, 0, KD))
+    W_PARTS = ((1, 3, 0, 512), (1, 3, 512, KD - 512), (0, 1, 0, KD))
 
     def w_copy(part, d):
         m0, m1, row, count_ = W_PARTS[part]
@@ -160,7 +160,7 @@
         piece = ebuf.at[k, rows_of(xl_, (z - d) % 8), :]
         return remote(piece, piece, ac_s.at[s, d], ac_r.at[s, d], core_sib)
 
-    order = (1, 7, 2, 6, 3, 5, 4)
+    order = (1, 7, 2)
     for d in order:
         az_copy(d).start()
     ax_copy(0).start()
@@ -412,6 +412,8 @@
         return s < 3 or (s == 3 and p == 2)
 
     def ring_step(b, s):
+        for near in ((0,), (7, 1), (6, 2), (5, 3))[s - 1]:
+            swap_land(b, near)
         for p in range(3):
             if goes_right(s - 1, p):
                 zr_copy(b, s - 1, p).wait_recv()
@@ -425,34 +427,41 @@
                 share(b, 8 - s, p)
             if goes_left(s - 1, p) and s < 4 or s == 4 and p == 2:
                 share(b, s, p)
-        if s == 2:
-            swap_land(b, 0)
-        if s > 2:
-            swap_land(b, 8 - (s - 2))
-            swap_land(b, s - 2)
-
-    def ring_end(b):
-        for s in (5, 3, 4):
-            swap_land(b, s)
-        for s in range(8):
+
+    odd_z = z % 2
+    PAIRS = (
+        (z // 2, 0, (1 + 6 * odd_z) % 8),
+        ((z // 2 + 3 + 2 * odd_z) % 4, (7 + 2 * odd_z) % 8, (6 + 4 * odd_z) % 8),
+        ((z // 2 + 5 - 2 * odd_z) % 4, (2 + 4 * odd_z) % 8, (3 + 2 * odd_z) % 8),
+        ((z // 2 + 2) % 4, 4, (5 + 6 * odd_z) % 8),
+    )
+
+    def pair_land(b, j):
+        for s in PAIRS[j][1:]:
             for h in range(2):
                 sib_copy(b, s, h).wait_recv()
             sib2_copy(b, s).wait_recv()
 
-    def scale(b, ys):
+    def unit(b, j):
+        pair_land(b, j)
+        ys = PAIRS[j][0]
         gain2 = g2[pl.ds(pl.multiple_of((4 * xh + ys) * KD, KD), KD)].reshape(1, KD)
         cols = pl.ds(pl.multiple_of(ys * KD, KD), KD)
         for r in range(3):
             rows = slice(r * 128, (r + 1) * 128)
             part = mall[b, rows, cols].astype(F32)
             squares_ = jnp.broadcast_to(jnp.sum(part * part, axis=1, keepdims=True), (128, 128))
-            ssb[b, rows, :] = squares_ if ys == 0 else ssb[b, rows, :] + squares_
+            ssb[b, rows, :] = squares_ if j == 0 else ssb[b, rows, :] + squares_
             xs[b, rows, cols] = (part * gain2).astype(BF16)
-
-    def project(pairs):
-        terms = [dot(xs[b], w2all[m].reshape(4 * KD, C)) for b, m in pairs]
-        for (b, m), term in zip(pairs, terms):
-            pp[b, :, m * C : (m + 1) * C] = term
+        for m in (1, 2):
+            lanes = slice(m * C, (m + 1) * C)
+            term = dot(xs[b, :, cols], w2all[m, ys])
+            pp[b, :, lanes] = term if j == 0 else pp[b, :, lanes] + term
+
+    def project_queries():
+        terms = [dot(xs[b], w2all[0].reshape(4 * KD, C)) for b in range(2)]
+        for b in range(2):
+            pp[b, :, :C] = terms[b]
 
     def g_copy(b, m):
         if m == 3:
@@ -513,44 +522,46 @@
     def finish_q(b):
         qbuf[b] = head_norm(joined(b, 0))
 
-    for h in range(2):
-        for b in range(2):
-            ring_start(b, h)
+    ring_start(0, 0)
+    ring_start(0, 1)
     ring_step(0, 1)
-    ring_step(1, 1)
+    ring_start(1, 0)
+    ring_start(1, 1)
     ring_step(0, 2)
     w_pass(1)
     w_send(2)
+    ring_step(0, 3)
+    ring_step(1, 1)
+    ring_step(0, 4)
     ring_step(1, 2)
-    ring_step(0, 3)
-    ring_step(1, 3)
-    ring_step(0, 4)
-    ring_step(1, 4)
-    ring_end(0)
-    for ys in range(4):
-        scale(0, ys)
-    send_squares(0)
     w_local.wait()
     w_land(0)
     w_land(1)
-    project(((0, 1), (0, 2)))
+    unit(0, 0)
+    swap_land(0, 4)
+    unit(0, 1)
+    unit(0, 2)
+    ring_step(1, 3)
+    unit(0, 3)
+    send_squares(0)
     send_half(0, (1, 2))
+    unit(1, 0)
     w_pass(2)
-    ring_end(1)
-    for ys in range(4):
-        scale(1, ys)
+    ring_step(1, 4)
+    unit(1, 1)
+    swap_land(1, 4)
+    unit(1, 2)
+    unit(1, 3)
     send_squares(1)
-    project(((1, 1), (1, 2)))
     send_half(1, (1, 2))
     finish_kv(0)
     w_land(2)
-    project(((0, 0), (1, 0)))
+    project_queries()
     send_half(0, (0,))
-    send_half(1, (0,))
     kv_pass(0)
     finish_kv(1)
+    send_half(1, (0,))
     finish_q(0)
-    finish_q(1)
     kv_land(0)
 
     factor = 2.0 * HEAD ** -0.5 * math.log2(math.e)
@@ -608,14 +619,15 @@
     earlier(0)
     conclude(0)
     kv_pass(1)
+    finish_q(1)
     key_block(1, 0, 0, first=True)
 
     @pl.loop(1, 4)
     def _(ys):
         key_block(1, ys, 0)
 
+    key_block(1, y, 1, diagonal=True)
     kv_land(1)
-    key_block(1, y, 1, diagonal=True)
     earlier(1)
     conclude(1)
     for chunk in range(3):
@@ -647,7 +659,7 @@
             w_forward(part, d).wait_send()
     for d in order:
         az_copy(d).wait_send()
-    for d in range(8):
+    for d in (0,) + order:
         ax_copy(d).wait_send()
         ac_copy(d, 0).wait_send()
         ac_copy(d, 1).wait_send()

time: 126 us -> 120 us (0.952)
  Pallas kernels: 125 us -> 119 us
    pallas_call x1, Pallas kernels: 123 us -> 117 us  [local(): pl.pallas_call(kernel, out_shape=(jax.ShapeDtypeStruct((T, C), BF16), jax...]
where the time goes in v4:
time: 120 us
  Pallas kernels  119 us (99%)
    pallas_call x1, Pallas kernels, local(): pl.pallas_call(kernel, out_shape=(jax.ShapeDtypeStruct((T, C), BF16), jax...  117 us

profile of v4, /device:TPU:28, one launch (start us, length us, event | category | flops | bytes accessed | tf_op | source)
XLA Modules:
  0.0 119.7 jit_solution(9131017357250163721)
XLA Ops:
  0.6 117.3 %shard_map.95 = (bf16[384,256]{1,0:T(8,128)(2,1)}, bf16[384,256]{1,0:T(8,128)(2,1)}) custom-call(s32[384]{0:T(512)} %ids.1, bf16[512,256]{1,0:T(8,128)(2,1)} %emb.1, f32[8192]{0:T(1024)} %g1.1, bf16[3,1024,256]{2,1,0:T(8,128)(2,1)} %bitcast.2, f32[3,3,256]{2,1,0:T(4,128)} %sf.1, f32[128,256]{1,0:T(8,128)} %lf.1, f32[8192]{0:T(1024)} %g2.1, ...), custom_call_target="tpu_custom_call" | custom-call | tf_op jit(solution)/shard_map/pallas_call | solution.py:754
  117.9 1.8 %shard_map.96 = (bf16[384,256]{1,0:T(8,128)(2,1)}, bf16[384,256]{1,0:T(8,128)(2,1)}) custom-call(bf16[384,256]{1,0:T(8,128)(2,1)} %get-tuple-element.4.mixed, bf16[384,256]{1,0:T(8,128)(2,1)} %get-tuple-element.5.att), custom_call_target="tpu_custom_call" | custom-call | tf_op jit(solution)/shard_map/pallas_call | solution.py:774

commit v5 on v4

--- a/solution.py
+++ b/solution.py
@@ -27,7 +27,7 @@
     ids, emb, g1, w1, sf, lf, g2, w2,
     mixed_out, att_out,
     idbuf, ebuf, xbuf, pkv, pq, psq, rskv, rsq, rssq, tkv, tq, sbuf, prbuf, taps, coef, xo, xu, xsum, dv, lcbuf, mbuf,
-    w2all, mall, xs, pp, ssb, gs, gr, sqs, sqr, qbuf, kvall, num, den, oloc, obuf,
+    w2all, mall, xs, pp, ssb, gs, gr, sqs, sqr, qbuf, kt, vv, num, den, oloc, obuf,
     id_s, id_r, sc_s, sc_r, az_s, az_r, ax_s, ax_r, ac_s, ac_r,
     rs_s, rs_r, ag_s, ag_r, w_s, w_r, wl_s, e1_s, e1_r, zr_s, zr_r, zl_s, zl_r, sw_s, sw_r, sib_s, sib_r,
     g_s, g_r, kv_s, kv_r, o_s, o_r,
@@ -98,7 +98,7 @@
         def _():
             cp.start()
 
-    W_PARTS = ((1, 3, 0, 512), (1, 3, 512, KD - 512), (0, 1, 0, KD))
+    W_PARTS = ((1, 3, 0, 512), (1, 3, 512, 512), (0, 1, 0, 512), (0, 1, 512, 512))
 
     def w_copy(part, d):
         m0, m1, row, count_ = W_PARTS[part]
@@ -292,7 +292,7 @@
         return pl.ds(pl.multiple_of((z_ * 2 + k_) * C + h * 128, 128), 128)
 
     def rows_at(h, half):
-        return pl.ds(0, T) if h == 0 else pl.ds(pl.multiple_of(half * (T // 2), T // 2), T // 2)
+        return pl.ds(0, T) if h == 1 else pl.ds(pl.multiple_of(half * (T // 2), T // 2), T // 2)
 
     def e1_copy(a, h):
         dst = mall.at[xh, rows_at(h, a), cols_of(z, k, h)]
@@ -364,8 +364,8 @@
     e1_send(1)
 
     def chunk_of(b, z_, p):
-        rows = rows_at(1, xl) if p == 2 else pl.ds(p * (T // 2), T // 2)
-        return mall.at[b, rows, cols_of(z_, k, p // 2)]
+        rows = rows_at(0, xl) if p == 2 else pl.ds(p * (T // 2), T // 2)
+        return mall.at[b, rows, cols_of(z_, k, 1 - p // 2)]
 
     def zr_copy(b, s, p):
         piece = chunk_of(b, (z + 8 - s) % 8, p)
@@ -380,16 +380,16 @@
         return remote(piece, piece, sib_s.at[b, s, h], sib_r.at[b, s, h], core_sib)
 
     def swap_copy(b, s):
-        piece = mall.at[b, rows_at(1, xl), cols_of((z + s) % 8, k, 1)]
+        piece = mall.at[b, rows_at(0, xl), cols_of((z + s) % 8, k, 0)]
         return remote(piece, piece, sw_s.at[b, s], sw_r.at[b, s], x_sib)
 
     def sib2_copy(b, s):
-        piece = mall.at[b, rows_at(1, 1 - xl), cols_of((z + s) % 8, k, 1)]
+        piece = mall.at[b, rows_at(0, 1 - xl), cols_of((z + s) % 8, k, 0)]
         return remote(piece, piece, sib_s.at[b, s, 2], sib_r.at[b, s, 2], core_sib)
 
     def share(b, s, p):
         if p > 0:
-            sib_copy(b, s, p - 1).start()
+            sib_copy(b, s, 2 - p).start()
         if p == 2:
             swap_copy(b, s).start()
 
@@ -400,10 +400,10 @@
     def ring_start(b, h):
         piece = mall.at[b, rows_at(h, xl), cols_of(z, k, h)]
         remote(piece, piece, e1_s.at[0, h], e1_r.at[b, h], core_sib).wait_recv()
-        for p in ((0, 1), (2,))[h]:
+        for p in ((2,), (0, 1))[h]:
             zr_copy(b, 0, p).start()
             zl_copy(b, 0, p).start()
-        share(b, 0, h + 1)
+        share(b, 0, 2 - h)
 
     def goes_right(s, p):
         return s < 3 or (s == 3 and p < 2)
@@ -414,7 +414,7 @@
     def ring_step(b, s):
         for near in ((0,), (7, 1), (6, 2), (5, 3))[s - 1]:
             swap_land(b, near)
-        for p in range(3):
+        for p in (2, 0, 1):
             if goes_right(s - 1, p):
                 zr_copy(b, s - 1, p).wait_recv()
                 if goes_right(s, p):
@@ -489,20 +489,22 @@
         values = values.astype(F32)
         return (values * lax.rsqrt(jnp.mean(values * values, axis=1, keepdims=True) + EPS)).astype(BF16)
 
-    def kv_copy(b, d):
-        block = kvall.at[y, b]
+    def kv_copy(b, d, part):
+        block = (kt, vv)[part].at[y, b]
         side = {1: 0, -1: 1}[d]
-        return remote(block, block, kv_s.at[b, side], kv_r.at[b, side], y_peer(d))
+        return remote(block, block, kv_s.at[b, part, side], kv_r.at[b, part, side], y_peer(d))
 
     def kv_forward(b, d):
         side = {1: 0, -1: 1}[d]
-        part = kvall.at[(y + 4 - d) % 4, b, side]
-        return remote(part, part, kv_s.at[b, 2 + side], kv_r.at[b, 2 + side], y_peer(d))
+        part = (kt, vv)[side].at[(y + 4 - d) % 4, b]
+        return remote(part, part, kv_s.at[b, 2, side], kv_r.at[b, 2, side], y_peer(d))
 
     def kv_pass(b):
         for d in (1, -1):
-            kv_copy(b, d).wait_recv()
+            kv_copy(b, d, 0 if d == 1 else 1).wait_recv()
             kv_forward(b, d).start()
+        for d in (1, -1):
+            kv_copy(b, d, 1 if d == 1 else 0).wait_recv()
 
     def kv_land(b):
         for d in (1, -1):
@@ -514,10 +516,11 @@
 
     def finish_kv(b):
         row_factor(b)
-        kvall[y, b, 0] = head_norm(joined(b, 1))
-        kvall[y, b, 1] = joined(b, 2)
-        for d in (1, -1):
-            kv_copy(b, d).start()
+        kt[y, b] = jnp.transpose(head_norm(joined(b, 1)))
+        vv[y, b] = joined(b, 2)
+        for part in range(2):
+            for d in (1, -1):
+                kv_copy(b, d, part).start()
 
     def finish_q(b):
         qbuf[b] = head_norm(joined(b, 0))
@@ -532,6 +535,7 @@
     w_send(2)
     ring_step(0, 3)
     ring_step(1, 1)
+    w_send(3)
     ring_step(0, 4)
     ring_step(1, 2)
     w_local.wait()
@@ -542,20 +546,22 @@
     unit(0, 1)
     unit(0, 2)
     ring_step(1, 3)
+    w_pass(2)
     unit(0, 3)
     send_squares(0)
     send_half(0, (1, 2))
     unit(1, 0)
-    w_pass(2)
     ring_step(1, 4)
     unit(1, 1)
+    w_pass(3)
+    finish_kv(0)
     swap_land(1, 4)
     unit(1, 2)
     unit(1, 3)
     send_squares(1)
     send_half(1, (1, 2))
-    finish_kv(0)
     w_land(2)
+    w_land(3)
     project_queries()
     send_half(0, (0,))
     kv_pass(0)
@@ -570,9 +576,7 @@
         for qc in range(3):
             rows = slice(qc * 128, (qc + 1) * 128)
             width = (qc + 1) * 128 if diagonal else T
-            score = lax.dot_general(
-                qbuf[b, rows, :], kvall[ys, kb, 0, :width, :], (((1,), (1,)), ((), ())), preferred_element_type=F32
-            )
+            score = dot(qbuf[b, rows, :], kt[ys, kb, :, :width])
             weight = jnp.exp2(score * factor)
             if diagonal:
                 at = qc * 128 + lax.broadcasted_iota(jnp.int32, (128, width), 0)
@@ -581,7 +585,7 @@
             part = weight[:, :128]
             for n in range(1, width // 128):
                 part = part + weight[:, n * 128 : (n + 1) * 128]
-            term = dot(weight.astype(BF16), kvall[ys, kb, 1, :width, :])
+            term = dot(weight.astype(BF16), vv[ys, kb, :width, :])
             if first:
                 den[b, rows, :] = part
                 num[b, rows, :] = term
@@ -653,7 +657,7 @@
             for h in range(2):
                 e1_copy(a, h)[2].wait_send()
 
-    for part in range(3):
+    for part in range(4):
         for d in (1, -1):
             w_copy(part, d).wait_send()
             w_forward(part, d).wait_send()
@@ -683,7 +687,8 @@
         for m in range(4):
             g_copy(b, m).wait_send()
         for d in (1, -1):
-            kv_copy(b, d).wait_send()
+            for part in range(2):
+                kv_copy(b, d, part).wait_send()
             kv_forward(b, d).wait_send()
     for chunk in range(3):
         o_copy(0, chunk).wait_send()
@@ -729,7 +734,8 @@
         vmem((2, 1, T), F32),
         vmem((2, 1, T), F32),
         vmem((2, T, HEAD), BF16),
-        vmem((4, 2, 2, T, HEAD), BF16),
+        vmem((4, 2, HEAD, T), BF16),
+        vmem((4, 2, T, HEAD), BF16),
         vmem((2, T, HEAD), F32),
         vmem((2, T, HEAD), F32),
         vmem((2, T, HEAD), BF16),
@@ -741,14 +747,14 @@
         dma((2, 8)), dma((2, 8)),
         dma((3, 2, 4)), dma((3, 8)),
         dma((2, 7)), dma((2, 7)),
-        dma((3, 2, 2)), dma((3, 2, 2)), dma,
+        dma((4, 2, 2)), dma((4, 2, 2)), dma,
         dma((2, 2)), dma((2, 2)),
         dma((2, 4, 3)), dma((2, 4, 3)),
         dma((2, 4, 3)), dma((2, 4, 3)),
         dma((2, 8)), dma((2, 8)),
         dma((2, 8, 3)), dma((2, 8, 3)),
         dma((2, 4)), dma((2, 4)),
-        dma((2, 4)), dma((2, 4)),
+        dma((2, 3, 2)), dma((2, 3, 2)),
         dma((3,)), dma((3,)),
     ]
     results = pl.pallas_call(

time: 120 us -> 118 us (0.983)
  Pallas kernels: 119 us -> 117 us
    pallas_call x1, Pallas kernels: 117 us -> 115 us  [local(): pl.pallas_call(kernel, out_shape=(jax.ShapeDtypeStruct((T, C), BF16), jax...]
where the time goes in v5:
time: 118 us
  Pallas kernels  117 us (99%)
    pallas_call x1, Pallas kernels, local(): pl.pallas_call(kernel, out_shape=(jax.ShapeDtypeStruct((T, C), BF16), jax...  115 us

profile of v5, /device:TPU:28, one launch (start us, length us, event | category | flops | bytes accessed | tf_op | source)
XLA Modules:
  0.0 117.9 jit_solution(16754839888598252103)
XLA Ops:
  0.6 115.4 %shard_map.95 = (bf16[384,256]{1,0:T(8,128)(2,1)}, bf16[384,256]{1,0:T(8,128)(2,1)}) custom-call(s32[384]{0:T(512)} %ids.1, bf16[512,256]{1,0:T(8,128)(2,1)} %emb.1, f32[8192]{0:T(1024)} %g1.1, bf16[3,1024,256]{2,1,0:T(8,128)(2,1)} %bitcast.2, f32[3,3,256]{2,1,0:T(4,128)} %sf.1, f32[128,256]{1,0:T(8,128)} %lf.1, f32[8192]{0:T(1024)} %g2.1, ...), custom_call_target="tpu_custom_call" | custom-call | tf_op jit(solution)/shard_map/pallas_call | solution.py:760
  116.1 1.8 %shard_map.96 = (bf16[384,256]{1,0:T(8,128)(2,1)}, bf16[384,256]{1,0:T(8,128)(2,1)}) custom-call(bf16[384,256]{1,0:T(8,128)(2,1)} %get-tuple-element.4.mixed, bf16[384,256]{1,0:T(8,128)(2,1)} %get-tuple-element.5.att), custom_call_target="tpu_custom_call" | custom-call | tf_op jit(solution)/shard_map/pallas_call | solution.py:780

commit v6 on v5

--- a/solution.py
+++ b/solution.py
@@ -554,8 +554,8 @@
     ring_step(1, 4)
     unit(1, 1)
     w_pass(3)
+    swap_land(1, 4)
     finish_kv(0)
-    swap_land(1, 4)
     unit(1, 2)
     unit(1, 3)
     send_squares(1)

time: 118 us -> 118 us (level)
  no operation moved by 1% of the time
where the time goes in v6:
time: 118 us
  Pallas kernels  117 us (99%)
    pallas_call x1, Pallas kernels, local(): pl.pallas_call(kernel, out_shape=(jax.ShapeDtypeStruct((T, C), BF16), jax...  115 us

profile of v6, /device:TPU:28, one launch (start us, length us, event | category | flops | bytes accessed | tf_op | source)
XLA Modules:
  0.0 117.6 jit_solution(10935318544303846425)
XLA Ops:
  0.6 115.2 %shard_map.95 = (bf16[384,256]{1,0:T(8,128)(2,1)}, bf16[384,256]{1,0:T(8,128)(2,1)}) custom-call(s32[384]{0:T(512)} %ids.1, bf16[512,256]{1,0:T(8,128)(2,1)} %emb.1, f32[8192]{0:T(1024)} %g1.1, bf16[3,1024,256]{2,1,0:T(8,128)(2,1)} %bitcast.2, f32[3,3,256]{2,1,0:T(4,128)} %sf.1, f32[128,256]{1,0:T(8,128)} %lf.1, f32[8192]{0:T(1024)} %g2.1, ...), custom_call_target="tpu_custom_call" | custom-call | tf_op jit(solution)/shard_map/pallas_call | solution.py:760
  115.9 1.8 %shard_map.96 = (bf16[384,256]{1,0:T(8,128)(2,1)}, bf16[384,256]{1,0:T(8,128)(2,1)}) custom-call(bf16[384,256]{1,0:T(8,128)(2,1)} %get-tuple-element.4.mixed, bf16[384,256]{1,0:T(8,128)(2,1)} %get-tuple-element.5.att), custom_call_target="tpu_custom_call" | custom-call | tf_op jit(solution)/shard_map/pallas_call | solution.py:780
